TPU v7x, 32 devices: a whole 2x2x4 slice. The times are simulated.
32 devices in a mesh: dp: 4 (over y, core), mp: 8 (over z, x).
Axes of the slice: x: 2, y: 2, z: 4, core: 2. Of those that a mesh axis runs over, the one named last changes fastest.
Arguments:
- hidden_rows: bfloat16 [768, 2048], P('dp'), may hold values from -6 to 6
- w_query: bfloat16 [2048, 2048], P(None, 'mp'), may hold values from -0.125 to 0.125
- w_key: bfloat16 [2048, 1024], P(None, 'mp'), may hold values from -0.125 to 0.125
- w_value: bfloat16 [2048, 1024], P(None, 'mp'), may hold values from -0.125 to 0.125
- w_out: bfloat16 [2048, 2048], P('mp'), may hold values from -0.125 to 0.125
- q_gain: float32 [128], replicated, may hold values from 0.25 to 1.75
- k_gain: float32 [128], replicated, may hold values from 0.25 to 1.75
- prefix_kv: bfloat16 [192, 2048], P('dp', 'mp')
- cotangent: bfloat16 [768, 2048], P('dp', 'mp'), may hold values from -6 to 6
- prompt_len: int32 [4], replicated, may hold values from 1 to 64, 192 in all
- resp_prompt: int32 [8], P('dp'), may hold values from 0 to 3
- resp_len: int32 [8], P('dp'), may hold values from 32 to 96, as said below
Outputs:
- mixed: bfloat16 [768, 2048], P('dp', 'mp')
- grad_input: bfloat16 [768, 2048], P('dp', 'mp')
- grad_prefix: bfloat16 [192, 2048], P('dp', 'mp')
Inputs may be any that keep to these rules, and one draw needn't show every extreme that they name: `prompt_len`: the lengths add up to 192; the longest is exactly 64. `resp_len`: some response of every draw has all 96 tokens live.
All inputs are finite; a program needn't handle non-finite values.
Results may differ from a plain program's by a relative error of at most 0.014.
The roundings to bfloat16 on the way count: a program that leaves them out, or rounds other values in their place, can miss the bound.
Values may be sent and summed in bfloat16 or wider, within the bound.
No kernel may reach another device: no remote copies, remote signals or barrier semaphores. Data moves between devices by JAX's collectives and lax.ppermute only.
A program may use at most 64 MiB of HBM per device.

v0:
```python
import functools

import jax
import jax.numpy as jnp
from jax import lax
from jax.experimental import pallas as pl
from jax.experimental.pallas import tpu as pltpu
from jax.sharding import PartitionSpec as P

EPS = 1e-06
NEG = -1e30
ROWS = 16
HELD = ((0,), (4, 2), (6,), (1,), (5, 3), (7,))
OUT = ((6, 7), (2, 3), (4, 5), (0, 1))
TERMS = ((1, 3), (0, 2))
IN = ((7, 5), (3,), (1,), (6,), (4,), (2,), (0,))
F32 = jnp.float32
BF16 = jnp.bfloat16
HBM = pl.BlockSpec(memory_space=pltpu.HBM)
SMEM = pl.BlockSpec(memory_space=pltpu.SMEM)
VMEM = pl.BlockSpec(memory_space=pltpu.VMEM)


def dot(left, right):
    return jnp.dot(left, right, preferred_element_type=F32)


def dot_nt(left, right):
    return lax.dot_general(left, right, (((1,), (1,)), ((), ())), preferred_element_type=F32)


def dot_tn(left, right):
    return lax.dot_general(left, right, (((0,), (0,)), ((), ())), preferred_element_type=F32)


def inverse_root(hidden):
    return lax.rsqrt(jnp.mean(hidden * hidden, axis=-1, keepdims=True) + EPS)


def norm_back(hidden, gain, grad):
    root = inverse_root(hidden)
    unit = hidden * root
    scaled = grad * gain
    return root * (scaled - unit * jnp.mean(scaled * unit, axis=-1, keepdims=True))


class Copies:
    def __init__(self, sems):
        self.sems, self.count = sems, 0

    def start(self, source, target):
        copy = pltpu.make_async_copy(source, target, self.sems.at[self.count])
        self.count += 1
        copy.start()
        return copy


def wait(copies):
    for copy in copies:
        copy.wait()


def prompt_span(prompt_len, prompt):
    first, last = 0, 0
    end = 0
    for p in range(prompt_len.shape[0]):
        begin = end
        end = end + prompt_len[p]
        first = jnp.where(prompt == p, begin, first)
        last = jnp.where(prompt == p, end, last)
    return first, last


def window_rows(count):
    return min(count, count // 3 + ROWS)


def window_start(first, count):
    start = jnp.minimum(first // ROWS * ROWS, count - window_rows(count))
    return pl.multiple_of(start, ROWS)


def slot_rows(slots, rows, step):
    if slots == 1:
        return pl.ds(0, rows)
    return pl.ds(pl.multiple_of((lax.axis_index("dp") ^ step) * rows, ROWS), rows)


def features(block, width):
    return pl.ds(pl.multiple_of(block * width, width), width)


def stacked(ref, rows, heads, size):
    return jnp.concatenate([ref[rows, a * size : (a + 1) * size] for a in heads], axis=0)


def make_blocks(make, names, refs):
    me = lax.axis_index("mp")
    for blocks, ref in zip(names, refs):
        for i, block in enumerate(blocks):
            ref[i] = make(features(me ^ block, ref.shape[-1]))


def taker(refs):
    refs = list(refs)

    def take(count):
        found, refs[:count] = refs[:count], []
        return found

    return take, refs


def project_kernel(*refs):
    take, _ = taker(refs)
    scalars = take(3)
    hidden, w_q, w_k, w_v, q_gain, k_gain, prefix, own = take(8)
    scalars_v = take(3)
    query, key, value, hq, hk = take(5)
    w_all, qg_v, kg_v, prefix_v, own_v = take(5)
    hidden_v, sems = take(2)

    copies = Copies(sems)
    depth = hidden.shape[1]
    steps = 4
    part = depth // steps
    places, end = [], 0
    for w in (w_q, w_k, w_v):
        places.append(slice(end, end + w.shape[1]))
        end += w.shape[1]
    loads = []
    for i in range(steps):
        cut = pl.ds(i * part, part)
        loads.append(
            [copies.start(hidden.at[:, cut], hidden_v.at[:, cut])]
            + [
                copies.start(w.at[cut], w_all.at[cut, place])
                for w, place in zip((w_q, w_k, w_v), places)
            ]
        )
    small = [copies.start(q_gain, qg_v), copies.start(k_gain, kg_v)]
    small += [copies.start(source, target) for source, target in zip(scalars, scalars_v)]
    small += [copies.start(prefix, prefix_v), copies.start(own, own_v)]

    whole = 0.0
    for i, load in enumerate(loads):
        wait(load)
        cut = slice(i * part, (i + 1) * part)
        whole += dot(hidden_v[:, cut], w_all[cut, :])
    hq[...], hk[...] = whole[:, places[0]], whole[:, places[1]]
    value[...] = whole[:, places[2]].astype(BF16)
    wait(small)
    size = qg_v.shape[1]
    for ref, gain, out in ((hq, qg_v, query), (hk, kg_v, key)):
        for at in range(0, ref.shape[1], size):
            head = ref[:, at : at + size]
            out[:, at : at + size] = (head * inverse_root(head) * gain[...]).astype(BF16)


def project(scalars, hidden, w_q, w_k, w_v, q_gain, k_gain, prefix, own):
    rows, depth = hidden.shape
    q_width, k_width = w_q.shape[1], w_k.shape[1]
    small = [q_gain, k_gain, prefix, own]
    operands = [*scalars, hidden, w_q, w_k, w_v, *small]
    kept = [
        ((rows, q_width), BF16),
        ((rows, k_width), BF16),
        ((rows, k_width), BF16),
        ((rows, q_width), F32),
        ((rows, k_width), F32),
        ((depth, q_width + 2 * k_width), BF16),
    ] + like(small)
    found = pl.pallas_call(
        project_kernel,
        in_specs=[HBM] * len(operands),
        out_specs=[SMEM] * 3 + [VMEM] * len(kept),
        out_shape=[pltpu.SMEM(x.shape, jnp.int32) for x in scalars] + in_vmem(kept),
        scratch_shapes=[pltpu.VMEM(hidden.shape, hidden.dtype), pltpu.SemaphoreType.DMA((32,))],
        compiler_params=pltpu.CompilerParams(vmem_limit_bytes=vmem_room(prefix.shape[0])),
        cost_estimate=lasting(2.6),
    )(*held_in(pltpu.HBM, operands))
    return found[:3], found[3:8], found[8:11], found[11], found[12]


def forward_kernel(slots, names, *refs):
    take, rest = taker(refs)
    prompt_len, resp_prompt, resp_len = take(3)
    query, key, value, wo_v = take(4)
    prefix = take(len(rest) - 4 - len(names) - 1)
    p_pre, p_own, heads_out, prefix_v = take(4)
    parts = take(len(names))
    (out_bf,) = take(1)

    held = prefix[0].shape[0]
    for k, ref in enumerate(prefix):
        prefix_v[slot_rows(len(prefix), held, k), :] = ref[...]
    size = heads_out.shape[1] * p_own.shape[3] // p_own.shape[2] // p_own.shape[1]
    count = prefix_v.shape[0]
    window = window_rows(count)
    slot_len = query.shape[0] // slots
    kv_heads = key.shape[1] // size
    groups = query.shape[1] // key.shape[1]
    scale = size ** (-0.5)
    for n in range(slots):
        first, last = prompt_span(prompt_len, resp_prompt[n])
        start = window_start(first, count)
        rows = slice(n * slot_len, (n + 1) * slot_len)
        live = lax.broadcasted_iota(jnp.int32, (slot_len, size), 0) < resp_len[n]
        for h in range(kv_heads):
            heads = range(h * groups, (h + 1) * groups)
            q = stacked(query, rows, heads, size)
            k_win = prefix_v[pl.ds(start, window), 2 * h * size : (2 * h + 1) * size]
            v_win = prefix_v[pl.ds(start, window), (2 * h + 1) * size : (2 * h + 2) * size]
            k_own = key[rows, h * size : (h + 1) * size]
            v_own = value[rows, h * size : (h + 1) * size]
            tall = groups * slot_len
            place = start + lax.broadcasted_iota(jnp.int32, (tall, window), 1)
            s_pre = jnp.where((place >= first) & (place < last), dot_nt(q, k_win) * scale, NEG)
            token = lax.broadcasted_iota(jnp.int32, (groups, slot_len, slot_len), 1)
            token = token.reshape(tall, slot_len)
            other = lax.broadcasted_iota(jnp.int32, (tall, slot_len), 1)
            s_own = jnp.where(
                (other <= token) & (other < resp_len[n]), dot_nt(q, k_own) * scale, NEG
            )
            top = jnp.maximum(
                jnp.max(s_pre, axis=-1, keepdims=True), jnp.max(s_own, axis=-1, keepdims=True)
            )
            e_pre = jnp.exp(s_pre - top)
            e_own = jnp.exp(s_own - top)
            total = jnp.sum(e_pre, axis=-1, keepdims=True) + jnp.sum(e_own, axis=-1, keepdims=True)
            b_pre = (e_pre / total).astype(BF16)
            b_own = (e_own / total).astype(BF16)
            p_pre[n, h] = b_pre
            p_own[n, h] = b_own
            out = dot(b_pre, v_win) + dot(b_own, v_own)
            for i, a in enumerate(heads):
                one = out[i * slot_len : (i + 1) * slot_len]
                heads_out[rows, a * size : (a + 1) * size] = one
                out_bf[rows, a * size : (a + 1) * size] = jnp.where(live, one, 0.0).astype(BF16)

    def make(cols):
        return dot(out_bf[...], wo_v[:, cols]).astype(BF16)

    make_blocks(make, names, parts)


def block_shapes(names, rows, width):
    return [((len(blocks), rows, width), BF16) for blocks in names]


def in_vmem(shapes):
    return [pltpu.VMEM(*x) for x in shapes]


def held_in(space, arrays):
    return [pltpu.with_memory_space_constraint(x, space) for x in arrays]


def lasting(us):
    return pl.CostEstimate(flops=int(us * 1.15e9), bytes_accessed=0, transcendentals=0)


def like(arrays):
    return [(x.shape, x.dtype) for x in arrays]


def vmem_room(prefix_rows):
    return 48 << 20 if prefix_rows > 1024 else 24 << 20


def forward(names, width, size, scalars, query, key, value, w_out, prefix):
    slots = scalars[-1].shape[0]
    rows, q_width = query.shape
    k_width = key.shape[1]
    count = sum(x.shape[0] for x in prefix)
    window = window_rows(count)
    slot_len = rows // slots
    kv_heads, tall = k_width // size, slot_len * q_width // k_width
    results = [
        ((slots, kv_heads, tall, window), BF16),
        ((slots, kv_heads, tall, slot_len), BF16),
        ((rows, q_width), F32),
        ((count, prefix[0].shape[1]), BF16),
    ] + block_shapes(names, rows, width)
    operands = [query, key, value, w_out, *prefix]
    found = pl.pallas_call(
        functools.partial(forward_kernel, slots, names),
        in_specs=[SMEM] * 3 + [VMEM] * len(operands),
        out_specs=[VMEM] * len(results),
        out_shape=in_vmem(results),
        scratch_shapes=[pltpu.VMEM((rows, q_width), BF16)],
        compiler_params=pltpu.CompilerParams(vmem_limit_bytes=vmem_room(count)),
        cost_estimate=lasting(1.7),
    )(*held_in(pltpu.SMEM, scalars), *held_in(pltpu.VMEM, operands))
    return found[:4], found[4:]


def backward_kernel(slots, names, *refs):
    take, rest = taker(refs)
    prompt_len, resp_prompt, resp_len = take(3)
    cotangent = take(len(HELD))
    query, key, value, hq, hk = take(5)
    w_all, q_gain, k_gain, w_out = take(4)
    p_pre, p_own, heads_out, prefix_v = take(4)
    terms = take(len(rest) - len(names) - 2)
    parts = take(len(names))
    grad_prefix, grads = take(2)

    width = cotangent[0].shape[2]
    me = lax.axis_index("mp")
    grad_heads = 0.0
    for blocks, ref in zip(HELD, cotangent):
        for i, block in enumerate(blocks):
            grad_heads += dot_nt(ref[i], w_out[:, features(me ^ block, width)])
    grad_prefix[...] = jnp.zeros_like(grad_prefix)

    count = prefix_v.shape[0]
    window = window_rows(count)
    slot_len = query.shape[0] // slots
    size = q_gain.shape[1]
    kv_heads = key.shape[1] // size
    groups = query.shape[1] // key.shape[1]
    scale = size ** (-0.5)
    for n in range(slots):
        first, _ = prompt_span(prompt_len, resp_prompt[n])
        start = window_start(first, count)
        rows = slice(n * slot_len, (n + 1) * slot_len)
        live = lax.broadcasted_iota(jnp.int32, (slot_len, size), 0) < resp_len[n]
        for h in range(kv_heads):
            heads = range(h * groups, (h + 1) * groups)
            q = stacked(query, rows, heads, size)
            out = stacked(heads_out, rows, heads, size)
            g = jnp.concatenate(
                [
                    jnp.where(live, grad_heads[rows, a * size : (a + 1) * size], 0.0).astype(BF16)
                    for a in heads
                ],
                axis=0,
            )
            k_win = prefix_v[pl.ds(start, window), 2 * h * size : (2 * h + 1) * size]
            v_win = prefix_v[pl.ds(start, window), (2 * h + 1) * size : (2 * h + 2) * size]
            k_own = key[rows, h * size : (h + 1) * size]
            v_own = value[rows, h * size : (h + 1) * size]
            b_pre, b_own = p_pre[n, h], p_own[n, h]
            delta = jnp.sum(g.astype(F32) * out, axis=-1, keepdims=True)
            ds_pre = (b_pre.astype(F32) * (dot_nt(g, v_win) - delta)).astype(BF16)
            ds_own = (b_own.astype(F32) * (dot_nt(g, v_own) - delta)).astype(BF16)
            grad_q = scale * (dot(ds_pre, k_win) + dot(ds_own, k_own))
            for i, a in enumerate(heads):
                cols = slice(a * size, (a + 1) * size)
                one = grad_q[i * slot_len : (i + 1) * slot_len]
                grads[rows, cols] = norm_back(hq[rows, cols], q_gain[...], one).astype(BF16)
            cols = slice(h * size, (h + 1) * size)
            q_width, k_width = query.shape[1], key.shape[1]
            key_cols = slice(q_width + h * size, q_width + (h + 1) * size)
            value_cols = slice(q_width + k_width + h * size, q_width + k_width + (h + 1) * size)
            grad_k = scale * dot_tn(ds_own, q)
            grads[rows, key_cols] = norm_back(hk[rows, cols], k_gain[...], grad_k).astype(BF16)
            grads[rows, value_cols] = dot_tn(b_own, g).astype(BF16)
            k_cols = slice(2 * h * size, (2 * h + 1) * size)
            v_cols = slice((2 * h + 1) * size, (2 * h + 2) * size)
            grad_prefix[pl.ds(start, window), k_cols] += scale * dot_tn(ds_pre, q)
            grad_prefix[pl.ds(start, window), v_cols] += dot_tn(b_pre, g)
    chips = prefix_v.shape[0] // terms[0].shape[1] if len(terms) > 1 else 1
    for ref, steps in zip(terms, TERMS if len(terms) > 1 else ((0,),)):
        for i, step in enumerate(steps):
            ref[i] = grad_prefix[slot_rows(chips, ref.shape[1], step), :]

    def make(cols):
        return dot_nt(grads[...], w_all[cols, :]).astype(BF16)

    make_blocks(make, names, parts)


def backward(names, scalars, cotangent, kept, terms):
    slots = scalars[-1].shape[0]
    query, key, w_out, prefix = kept[0], kept[1], kept[8], kept[12]
    rows, q_width = query.shape
    k_width = key.shape[1]
    count, kv_width = prefix.shape
    results = [(x, F32) for x in terms] + block_shapes(names, rows, cotangent[0].shape[2])
    found = pl.pallas_call(
        functools.partial(backward_kernel, slots, names),
        in_specs=[SMEM] * 3 + [VMEM] * (len(cotangent) + len(kept)),
        out_specs=[VMEM] * len(results),
        out_shape=in_vmem(results),
        scratch_shapes=[
            pltpu.VMEM((count, kv_width), F32),
            pltpu.VMEM((rows, q_width + 2 * k_width), BF16),
        ],
        compiler_params=pltpu.CompilerParams(vmem_limit_bytes=vmem_room(count)),
        cost_estimate=lasting(3.5),
    )(*held_in(pltpu.SMEM, scalars), *held_in(pltpu.VMEM, [*cotangent, *kept]))
    return found[: len(terms)], found[len(terms) :]


def last_kernel(counts, *refs):
    take, rest = taker(refs)
    groups = [take(len(count)) for count in counts]
    results = take(len(counts))
    stage = take(len(counts))
    (sems,) = take(1)
    copies = Copies(sems)
    stores = []
    for count, group, result, ref in zip(counts, groups, results, stage):
        whole = 0.0
        for i, term in zip(count, group):
            whole = whole + term[i].astype(F32)
        ref[...] = whole.astype(BF16)
        stores.append(copies.start(ref, result))
    wait(stores)


def last_sums(groups):
    arrays = [array for group in groups for array, _ in group]
    shapes = [jax.ShapeDtypeStruct(group[0][0].shape[1:], BF16) for group in groups]
    return pl.pallas_call(
        functools.partial(last_kernel, [[i for _, i in group] for group in groups]),
        in_specs=[VMEM] * len(arrays),
        out_specs=[HBM] * len(groups),
        out_shape=shapes,
        scratch_shapes=in_vmem(like(shapes)) + [pltpu.SemaphoreType.DMA((len(groups),))],
        compiler_params=pltpu.CompilerParams(vmem_limit_bytes=vmem_room(0)),
        cost_estimate=lasting(0.9),
    )(*held_in(pltpu.VMEM, arrays))


def trade(name, block, axis, step):
    with jax.named_scope(name):
        return lax.ppermute(block, axis, [(i, i ^ step) for i in range(lax.axis_size(axis))])


def after(value, *others):
    return lax.optimization_barrier((value, *others))[0]


def total(*terms):
    whole = terms[0].astype(F32)
    for term in terms[1:]:
        whole = whole + term.astype(F32)
    return whole.astype(BF16)


def per_device(
    hidden_rows,
    w_query,
    w_key,
    w_value,
    w_out,
    q_gain,
    k_gain,
    prefix_kv,
    cotangent,
    prompt_len,
    resp_prompt,
    resp_len,
):
    chips = lax.axis_size("dp")
    scalars = (prompt_len, resp_prompt, resp_len)
    q_gain, k_gain = q_gain[None], k_gain[None]
    own = cotangent[None]
    far = trade("gather_far", own, "mp", 4)
    near = trade("gather_near", own, "mp", 2)
    if chips == 4:
        others = [trade("gather_prefix", prefix_kv, "dp", k) for k in range(1, chips)]
    else:
        prefix_kv, others = lax.all_gather(prefix_kv, "dp", axis=0, tiled=True), []
    far = after(far, *others)
    both = trade("gather_both", far, "mp", 2)
    pair = jnp.concatenate([far, near])
    pair_x = trade("gather_pair_x", pair, "mp", 1)
    own_x = trade("gather_own_x", own, "mp", 1)
    scalars, projected, weights, prefix, own = project(
        scalars, after(hidden_rows, far), w_query, w_key, w_value, q_gain, k_gain, prefix_kv, own
    )
    both_x = trade("gather_both_x", after(both, projected[0]), "mp", 1)
    probed, parts = forward(
        OUT, cotangent.shape[1], q_gain.shape[1], scalars, *projected[:3], w_out,
        [prefix, *others],
    )
    back = [own, pair, both, own_x, pair_x, both_x]
    shape = prefix_kv.shape
    terms = [(1, *shape)] if chips != 4 else [(len(steps), *shape) for steps in TERMS]
    terms, grads = backward(IN, scalars, back, [*projected, *weights, w_out, *probed], terms)

    out_a, out_b, kept_a, kept_b = parts
    got_a = trade("out_a", out_a, "mp", 2)
    got_b = trade("out_b", after(out_b, pair_x), "mp", 2)
    out_a = total(kept_a, got_a)
    got_out = trade("out_mid", out_a, "mp", 4)
    in_75, in_3, in_1, in_6, in_4, in_2, in_0 = grads
    got_75 = trade("in_75", in_75, "mp", 1)
    got_3 = trade("in_3", in_3, "mp", 1)
    in_6 = total(after(in_6, out_a), got_75[:1])
    got_6 = trade("in_6", in_6, "mp", 2)
    in_2 = total(in_2, got_3)
    got_2 = trade("in_2", in_2, "mp", 2)
    if chips == 4:
        got = trade("grad_prefix_core", after(terms[0], in_2), "dp", 1)
        last = trade("grad_prefix_y", terms[1][1:] + got[1:], "dp", 2)
    in_4 = total(after(in_4, got_b, got_out, in_2), got_75[1:], got_6)
    got_4 = trade("in_4", in_4, "mp", 4)
    got_1 = trade("in_1", after(in_1, in_4), "mp", 1)
    got_x = trade("out_x", total(after(kept_b, in_4)[1:], got_b[1:], got_out[1:]), "mp", 1)
    groups = [
        [(kept_b, 0), (got_b, 0), (got_out, 0), (got_x, 0)],
        [(in_0, 0), (got_1, 0), (got_2, 0), (got_4, 0)],
    ]
    if chips == 4:
        groups.append([(terms[1], 0), (got, 0), (last, 0)])
        return last_sums(groups)
    grad_prefix = lax.psum_scatter(terms[0][0], "dp", scatter_dimension=0, tiled=True)
    return *last_sums(groups), grad_prefix.astype(BF16)


def solution(mesh):
    in_specs = (
        P("dp", None),
        P(None, "mp"),
        P(None, "mp"),
        P(None, "mp"),
        P("mp", None),
        P(),
        P(),
        P("dp", "mp"),
        P("dp", "mp"),
        P(),
        P("dp"),
        P("dp"),
    )
    out_specs = (P("dp", "mp"), P("dp", "mp"), P("dp", "mp"))
    return jax.shard_map(
        per_device, mesh=mesh, in_specs=in_specs, out_specs=out_specs, check_vma=False
    )
```

profile of v0, /device:TPU:0, one launch (start us, length us, event | category | flops | bytes accessed | tf_op | source)
XLA Modules:
  0.0 44.7 jit_solution(4083130505838108514)
XLA Ops:
  0.6 4.1 %collective-permute-start = (bf16[1,192,256]{2,1,0:T(8,128)(2,1)}, bf16[1,192,256]{2,1,0:T(8,128)(2,1)S(1)}, u32[]{:S(2)}, u32[]{:S(2)}) collective-permute-start(bf16[1,192,256]{2,1,0:T(8,128)(2,1)} %bitcast.3), channel_id=1, source_target_pairs={{0,4},{1,5},{2,6},{3,7},{4,0},{5,1},{6,2},{7,3},{8,12},{9,13},{10,... | collective-permute-start | bytes 294920 | tf_op jit(solution)/shard_map/gather_far/ppermute | solution.py:430
  4.7 1.5 %collective-permute-start.2 = (bf16[48,256]{1,0:T(8,128)(2,1)}, bf16[48,256]{1,0:T(8,128)(2,1)S(1)}, u32[]{:S(2)}, u32[]{:S(2)}) collective-permute-start(bf16[48,256]{1,0:T(8,128)(2,1)} %refs_9_.1), channel_id=1, source_target_pairs={{0,16},{8,24},{16,0},{24,8},{1,17},{9,25},{17,1},{25,9},{2,18},{10... | collective-permute-start | bytes 73736 | tf_op jit(solution)/shard_map/gather_prefix/ppermute | solution.py:430
  6.6 1.6 %collective-permute-start.4 = (bf16[1,192,256]{2,1,0:T(8,128)(2,1)}, bf16[1,192,256]{2,1,0:T(8,128)(2,1)S(1)}, u32[]{:S(2)}, u32[]{:S(2)}) collective-permute-start(bf16[1,192,256]{2,1,0:T(8,128)(2,1)} %bitcast.4), channel_id=1, source_target_pairs={{0,2},{1,3},{2,0},{3,1},{4,6},{5,7},{6,4},{7,5},{8,10},{9,11},{10,... | collective-permute-start | bytes 294920 | tf_op jit(solution)/shard_map/gather_near/ppermute | solution.py:430
  8.2 1.5 %collective-permute-start.10 = (bf16[1,192,256]{2,1,0:T(8,128)(2,1)}, bf16[1,192,256]{2,1,0:T(8,128)(2,1)S(1)}, u32[]{:S(2)}, u32[]{:S(2)}) collective-permute-start(bf16[1,192,256]{2,1,0:T(8,128)(2,1)} %bitcast.5), channel_id=1, source_target_pairs={{0,1},{1,0},{2,3},{3,2},{4,5},{5,4},{6,7},{7,6},{8,9},{9,8},{10,11... | collective-permute-start | bytes 294920 | tf_op jit(solution)/shard_map/gather_own_x/ppermute | solution.py:430
  9.9 1.4 %collective-permute-start.9 = (bf16[1,192,256]{2,1,0:T(8,128)(2,1)S(1)}, bf16[1,192,256]{2,1,0:T(8,128)(2,1)S(1)}, u32[]{:S(2)}, u32[]{:S(2)}) collective-permute-start(bf16[1,192,256]{2,1,0:T(8,128)(2,1)S(1)} %collective-permute-done), channel_id=1, source_target_pairs={{0,2},{1,3},{2,0},{3,1},{4,6},{5,7},{6,4},{7,5},{8,10},{9,11},{10,... | collective-permute-start | bytes 294920 | tf_op jit(solution)/shard_map/gather_both/ppermute | solution.py:430
  12.0 1.6 %collective-permute-start.5 = (bf16[2,192,256]{2,1,0:T(8,128)(2,1)S(1)}, bf16[2,192,256]{2,1,0:T(8,128)(2,1)S(1)}, u32[]{:S(2)}, u32[]{:S(2)}) collective-permute-start(bf16[2,192,256]{2,1,0:T(8,128)(2,1)S(1)} %constant_dynamic-update-slice_fusion.refs_4_), channel_id=1, source_target_pairs={{0,1},{1,0},{2,3},{3,2},{4,5},{5,4},{6,7},{7,6},{8,9},{9,8},{10,11... | collective-permute-start | bytes 589832 | tf_op jit(solution)/shard_map/gather_pair_x/ppermute | solution.py:430
  13.6 2.6 %shard_map.139 = (s32[4]{0:T(128)S(4)}, s32[2]{0:T(128)S(4)}, s32[2]{0:T(128)S(4)}, bf16[192,256]{1,0:T(8,128)(2,1)S(1)}, bf16[192,128]{1,0:T(8,128)(2,1)S(1)}, ...) custom-call(s32[4]{0:T(128)} %refs_0_.1, ...), custom_call_target="tpu_custom_call" | custom-call | flops 2990000128 | tf_op jit(solution)/shard_map/pallas_call | solution.py:173
  16.8 1.0 %shard_map.140 = (bf16[2,1,192,80]{3,2,1,0:T(8,128)(2,1)S(1)}, bf16[2,1,192,96]{3,2,1,0:T(8,128)(2,1)S(1)}, f32[192,256]{1,0:T(8,128)S(1)}, bf16[192,256]{1,0:T(...) custom-call(s32[4]{0:T(128)S(4)} %get-tuple-element.44.refs_0_, ...), custom_call_target="tpu_custom_call" | custom-call | flops 1955000064 | tf_op jit(solution)/shard_map/pallas_call | solution.py:286
  17.7 1.5 %collective-permute-start.7 = (bf16[2,192,256]{2,1,0:T(8,128)(2,1)S(1)}, bf16[2,192,256]{2,1,0:T(8,128)(2,1)S(1)}, u32[]{:S(2)}, u32[]{:S(2)}) collective-permute-start(bf16[2,192,256]{2,1,0:T(8,128)(2,1)S(1)} %get-tuple-element.55), channel_id=1, source_target_pairs={{0,2},{1,3},{2,0},{3,1},{4,6},{5,7},{6,4},{7,5},{8,10},{9,11},{10,... | collective-permute-start | bytes 589832 | tf_op jit(solution)/shard_map/out_a/ppermute | solution.py:430
  19.9 1.0 %collective-permute-done.11.refs_8_ = bf16[1,192,256]{2,1,0:T(8,128)(2,1)S(1)} collective-permute-done((bf16[1,192,256]{2,1,0:T(8,128)(2,1)S(1)}, bf16[1,192,256]{2,1,0:T(8,128)(2,1)S(1)}, u32[]{:S(2)}, u32[]{:S(2)}) %collective-permute-start.11) | collective-permute-done | bytes 98336 | tf_op jit(solution)/shard_map/gather_both_x/ppermute | solution.py:430
  20.9 2.3 %shard_map.141 = (f32[2,48,256]{2,1,0:T(8,128)S(1)}, f32[2,48,256]{2,1,0:T(8,128)S(1)}, bf16[2,192,256]{2,1,0:T(8,128)(2,1)S(1)}, bf16[1,192,256]{2,1,0:T(8,128)...) custom-call(s32[4]{0:T(128)S(4)} %get-tuple-element.44.refs_0_, ...), custom_call_target="tpu_custom_call" | custom-call | flops 4024999936 | tf_op jit(solution)/shard_map/pallas_call | solution.py:382
  23.2 1.4 %collective-permute-start.13 = (bf16[2,192,256]{2,1,0:T(8,128)(2,1)S(1)}, bf16[2,192,256]{2,1,0:T(8,128)(2,1)S(1)}, u32[]{:S(2)}, u32[]{:S(2)}) collective-permute-start(bf16[2,192,256]{2,1,0:T(8,128)(2,1)S(1)} %get-tuple-element.71), channel_id=1, source_target_pairs={{0,1},{1,0},{2,3},{3,2},{4,5},{5,4},{6,7},{7,6},{8,9},{9,8},{10,11... | collective-permute-start | bytes 589832 | tf_op jit(solution)/shard_map/in_75/ppermute | solution.py:430
  24.7 1.0 %collective-permute-done.7 = bf16[2,192,256]{2,1,0:T(8,128)(2,1)S(1)} collective-permute-done((bf16[2,192,256]{2,1,0:T(8,128)(2,1)S(1)}, bf16[2,192,256]{2,1,0:T(8,128)(2,1)S(1)}, u32[]{:S(2)}, u32[]{:S(2)}) %collective-permute-start.7) | collective-permute-done | bytes 196640 | tf_op jit(solution)/shard_map/out_a/ppermute | solution.py:430
  25.7 2.2 %collective-permute-start.8 = (bf16[2,192,256]{2,1,0:T(8,128)(2,1)S(1)}, bf16[2,192,256]{2,1,0:T(8,128)(2,1)S(1)}, u32[]{:S(2)}, u32[]{:S(2)}) collective-permute-start(bf16[2,192,256]{2,1,0:T(8,128)(2,1)S(1)} %add_convert_fusion), channel_id=1, source_target_pairs={{0,4},{1,5},{2,6},{3,7},{4,0},{5,1},{6,2},{7,3},{8,12},{9,13},{10,... | collective-permute-start | bytes 589832 | tf_op jit(solution)/shard_map/out_mid/ppermute | solution.py:430
  27.9 1.5 %collective-permute-start.12 = (bf16[1,192,256]{2,1,0:T(8,128)(2,1)S(1)}, bf16[1,192,256]{2,1,0:T(8,128)(2,1)S(1)}, u32[]{:S(2)}, u32[]{:S(2)}) collective-permute-start(bf16[1,192,256]{2,1,0:T(8,128)(2,1)S(1)} %get-tuple-element.69), channel_id=1, source_target_pairs={{0,1},{1,0},{2,3},{3,2},{4,5},{5,4},{6,7},{7,6},{8,9},{9,8},{10,11... | collective-permute-start | bytes 294920 | tf_op jit(solution)/shard_map/in_3/ppermute | solution.py:430
  30.0 1.3 %collective-permute-start.14 = (bf16[1,192,256]{2,1,0:T(8,128)(2,1)S(1)}, bf16[1,192,256]{2,1,0:T(8,128)(2,1)S(1)}, u32[]{:S(2)}, u32[]{:S(2)}) collective-permute-start(bf16[1,192,256]{2,1,0:T(8,128)(2,1)S(1)} %add_convert_fusion.3), channel_id=1, source_target_pairs={{0,2},{1,3},{2,0},{3,1},{4,6},{5,7},{6,4},{7,5},{8,10},{9,11},{10,... | collective-permute-start | bytes 294920 | tf_op jit(solution)/shard_map/in_6/ppermute | solution.py:430
  31.3 1.2 %collective-permute-done.12 = bf16[1,192,256]{2,1,0:T(8,128)(2,1)S(1)} collective-permute-done((bf16[1,192,256]{2,1,0:T(8,128)(2,1)S(1)}, bf16[1,192,256]{2,1,0:T(8,128)(2,1)S(1)}, u32[]{:S(2)}, u32[]{:S(2)}) %collective-permute-start.12) | collective-permute-done | bytes 98336 | tf_op jit(solution)/shard_map/in_3/ppermute | solution.py:430
  32.5 1.7 %collective-permute-start.17 = (bf16[1,192,256]{2,1,0:T(8,128)(2,1)S(1)}, bf16[1,192,256]{2,1,0:T(8,128)(2,1)S(1)}, u32[]{:S(2)}, u32[]{:S(2)}) collective-permute-start(bf16[1,192,256]{2,1,0:T(8,128)(2,1)S(1)} %add_convert_fusion.4), channel_id=1, source_target_pairs={{0,2},{1,3},{2,0},{3,1},{4,6},{5,7},{6,4},{7,5},{8,10},{9,11},{10,... | collective-permute-start | bytes 294920 | tf_op jit(solution)/shard_map/in_2/ppermute | solution.py:430
  34.8 1.0 %collective-permute-done.14 = bf16[1,192,256]{2,1,0:T(8,128)(2,1)S(1)} collective-permute-done((bf16[1,192,256]{2,1,0:T(8,128)(2,1)S(1)}, bf16[1,192,256]{2,1,0:T(8,128)(2,1)S(1)}, u32[]{:S(2)}, u32[]{:S(2)}) %collective-permute-start.14) | collective-permute-done | bytes 98336 | tf_op jit(solution)/shard_map/in_6/ppermute | solution.py:430
  35.8 1.7 %collective-permute-start.18 = (bf16[1,192,256]{2,1,0:T(8,128)(2,1)S(1)}, bf16[1,192,256]{2,1,0:T(8,128)(2,1)S(1)}, u32[]{:S(2)}, u32[]{:S(2)}) collective-permute-start(bf16[1,192,256]{2,1,0:T(8,128)(2,1)S(1)} %add_convert_fusion.2), channel_id=1, source_target_pairs={{0,4},{1,5},{2,6},{3,7},{4,0},{5,1},{6,2},{7,3},{8,12},{9,13},{10,... | collective-permute-start | bytes 294920 | tf_op jit(solution)/shard_map/in_4/ppermute | solution.py:430
  37.6 1.5 %collective-permute-start.15 = (bf16[1,192,256]{2,1,0:T(8,128)(2,1)S(1)}, bf16[1,192,256]{2,1,0:T(8,128)(2,1)S(1)}, u32[]{:S(2)}, u32[]{:S(2)}) collective-permute-start(bf16[1,192,256]{2,1,0:T(8,128)(2,1)S(1)} %add_convert_fusion.1), channel_id=1, source_target_pairs={{0,1},{1,0},{2,3},{3,2},{4,5},{5,4},{6,7},{7,6},{8,9},{9,8},{10,11... | collective-permute-start | bytes 294920 | tf_op jit(solution)/shard_map/out_x/ppermute | solution.py:430
  39.7 1.6 %collective-permute-start.20 = (f32[1,48,256]{2,1,0:T(8,128)S(1)}, f32[1,48,256]{2,1,0:T(8,128)S(1)}, u32[]{:S(2)}, u32[]{:S(2)}) collective-permute-start(f32[1,48,256]{2,1,0:T(8,128)S(1)} %slice_add_fusion), channel_id=1, source_target_pairs={{0,16},{8,24},{16,0},{24,8},{1,17},{9,25},{17,1},{25,9},{2,18},{10... | collective-permute-start | bytes 147464 | tf_op jit(solution)/shard_map/grad_prefix_y/ppermute | solution.py:430
  41.3 2.6 %collective-permute-done.20.refs_10_ = f32[1,48,256]{2,1,0:T(8,128)S(1)} collective-permute-done((f32[1,48,256]{2,1,0:T(8,128)S(1)}, f32[1,48,256]{2,1,0:T(8,128)S(1)}, u32[]{:S(2)}, u32[]{:S(2)}) %collective-permute-start.20) | collective-permute-done | bytes 49184 | tf_op jit(solution)/shard_map/grad_prefix_y/ppermute | solution.py:430
  43.9 0.8 %shard_map.142 = (bf16[192,256]{1,0:T(8,128)(2,1)}, bf16[192,256]{1,0:T(8,128)(2,1)}, bf16[48,256]{1,0:T(8,128)(2,1)}) custom-call(bf16[2,192,256]{2,1,0:T(8,128)(2,1)S(1)} %get-tuple-element.74.refs_0_, bf16[2,192,256]{2,1,0:T(8,128)(2,1)S(1)} %collective-permute-done.6.refs_1_, bf16[2,192,256]{2,1,0:T(8,128)(2,1)S(1)} %collective-permute-done.8.refs_2_, ...), custom_call_target="tpu_custom_call" | custom-call | flops 1035000000 | tf_op jit(solution)/shard_map/pallas_call | solution.py:417
  (32 shorter events, 4.4 us)
Async XLA Ops:
  0.6 9.2 %collective-permute-start = (bf16[1,192,256]{2,1,0:T(8,128)(2,1)}, bf16[1,192,256]{2,1,0:T(8,128)(2,1)S(1)}, u32[]{:S(2)}, u32[]{:S(2)}) collective-permute-start(bf16[1,192,256]{2,1,0:T(8,128)(2,1)} %bitcast.3), channel_id=1, source_target_pairs={{0,4},{1,5},{2,6},{3,7},{4,0},{5,1},{6,2},{7,3},{8,12},{9,13},{10,... | collective-permute-start | bytes 294920 | tf_op jit(solution)/shard_map/gather_far/ppermute | solution.py:430
  4.7 3.4 %collective-permute-start.1 = (bf16[48,256]{1,0:T(8,128)(2,1)}, bf16[48,256]{1,0:T(8,128)(2,1)S(1)}, u32[]{:S(2)}, u32[]{:S(2)}) collective-permute-start(bf16[48,256]{1,0:T(8,128)(2,1)} %refs_9_.1), channel_id=1, source_target_pairs={{0,8},{8,0},{16,24},{24,16},{1,9},{9,1},{17,25},{25,17},{2,10},{10... | collective-permute-start | bytes 73736 | tf_op jit(solution)/shard_map/gather_prefix/ppermute | solution.py:430
  4.7 4.9 %collective-permute-start.2 = (bf16[48,256]{1,0:T(8,128)(2,1)}, bf16[48,256]{1,0:T(8,128)(2,1)S(1)}, u32[]{:S(2)}, u32[]{:S(2)}) collective-permute-start(bf16[48,256]{1,0:T(8,128)(2,1)} %refs_9_.1), channel_id=1, source_target_pairs={{0,16},{8,24},{16,0},{24,8},{1,17},{9,25},{17,1},{25,9},{2,18},{10... | collective-permute-start | bytes 73736 | tf_op jit(solution)/shard_map/gather_prefix/ppermute | solution.py:430
  6.3 3.5 %collective-permute-start.3 = (bf16[48,256]{1,0:T(8,128)(2,1)}, bf16[48,256]{1,0:T(8,128)(2,1)S(1)}, u32[]{:S(2)}, u32[]{:S(2)}) collective-permute-start(bf16[48,256]{1,0:T(8,128)(2,1)} %refs_9_.1), channel_id=1, source_target_pairs={{0,24},{8,16},{16,8},{24,0},{1,25},{9,17},{17,9},{25,1},{2,26},{10... | collective-permute-start | bytes 73736 | tf_op jit(solution)/shard_map/gather_prefix/ppermute | solution.py:430
  6.6 5.4 %collective-permute-start.4 = (bf16[1,192,256]{2,1,0:T(8,128)(2,1)}, bf16[1,192,256]{2,1,0:T(8,128)(2,1)S(1)}, u32[]{:S(2)}, u32[]{:S(2)}) collective-permute-start(bf16[1,192,256]{2,1,0:T(8,128)(2,1)} %bitcast.4), channel_id=1, source_target_pairs={{0,2},{1,3},{2,0},{3,1},{4,6},{5,7},{6,4},{7,5},{8,10},{9,11},{10,... | collective-permute-start | bytes 294920 | tf_op jit(solution)/shard_map/gather_near/ppermute | solution.py:430
  8.2 11.8 %collective-permute-start.10 = (bf16[1,192,256]{2,1,0:T(8,128)(2,1)}, bf16[1,192,256]{2,1,0:T(8,128)(2,1)S(1)}, u32[]{:S(2)}, u32[]{:S(2)}) collective-permute-start(bf16[1,192,256]{2,1,0:T(8,128)(2,1)} %bitcast.5), channel_id=1, source_target_pairs={{0,1},{1,0},{2,3},{3,2},{4,5},{5,4},{6,7},{7,6},{8,9},{9,8},{10,11... | collective-permute-start | bytes 294920 | tf_op jit(solution)/shard_map/gather_own_x/ppermute | solution.py:430
  9.9 6.3 %collective-permute-start.9 = (bf16[1,192,256]{2,1,0:T(8,128)(2,1)S(1)}, bf16[1,192,256]{2,1,0:T(8,128)(2,1)S(1)}, u32[]{:S(2)}, u32[]{:S(2)}) collective-permute-start(bf16[1,192,256]{2,1,0:T(8,128)(2,1)S(1)} %collective-permute-done), channel_id=1, source_target_pairs={{0,2},{1,3},{2,0},{3,1},{4,6},{5,7},{6,4},{7,5},{8,10},{9,11},{10,... | collective-permute-start | bytes 294920 | tf_op jit(solution)/shard_map/gather_both/ppermute | solution.py:430
  12.0 7.3 %collective-permute-start.5 = (bf16[2,192,256]{2,1,0:T(8,128)(2,1)S(1)}, bf16[2,192,256]{2,1,0:T(8,128)(2,1)S(1)}, u32[]{:S(2)}, u32[]{:S(2)}) collective-permute-start(bf16[2,192,256]{2,1,0:T(8,128)(2,1)S(1)} %constant_dynamic-update-slice_fusion.refs_4_), channel_id=1, source_target_pairs={{0,1},{1,0},{2,3},{3,2},{4,5},{5,4},{6,7},{7,6},{8,9},{9,8},{10,11... | collective-permute-start | bytes 589832 | tf_op jit(solution)/shard_map/gather_pair_x/ppermute | solution.py:430
  13.6 3.2 %copy-start = (bf16[256,2048]{1,0:T(8,128)(2,1)S(1)}, bf16[256,2048]{1,0:T(8,128)(2,1)}, u32[]{:S(2)}) copy-start(bf16[256,2048]{1,0:T(8,128)(2,1)} %refs_17_.1) | copy-start | bytes 3145732
  16.2 4.7 %collective-permute-start.11 = (bf16[1,192,256]{2,1,0:T(8,128)(2,1)S(1)}, bf16[1,192,256]{2,1,0:T(8,128)(2,1)S(1)}, u32[]{:S(2)}, u32[]{:S(2)}) collective-permute-start(bf16[1,192,256]{2,1,0:T(8,128)(2,1)S(1)} %collective-permute-done.9.refs_5_), channel_id=1, source_target_pairs={{0,1},{1,0},{2,3},{3,2},{4,5},{5,4},{6,7},{7,6},{8,9},{9,8},{10,11... | collective-permute-start | bytes 294920 | tf_op jit(solution)/shard_map/gather_both_x/ppermute | solution.py:430
  17.7 7.9 %collective-permute-start.7 = (bf16[2,192,256]{2,1,0:T(8,128)(2,1)S(1)}, bf16[2,192,256]{2,1,0:T(8,128)(2,1)S(1)}, u32[]{:S(2)}, u32[]{:S(2)}) collective-permute-start(bf16[2,192,256]{2,1,0:T(8,128)(2,1)S(1)} %get-tuple-element.55), channel_id=1, source_target_pairs={{0,2},{1,3},{2,0},{3,1},{4,6},{5,7},{6,4},{7,5},{8,10},{9,11},{10,... | collective-permute-start | bytes 589832 | tf_op jit(solution)/shard_map/out_a/ppermute | solution.py:430
  19.2 15.0 %collective-permute-start.6 = (bf16[2,192,256]{2,1,0:T(8,128)(2,1)S(1)}, bf16[2,192,256]{2,1,0:T(8,128)(2,1)S(1)}, u32[]{:S(2)}, u32[]{:S(2)}) collective-permute-start(bf16[2,192,256]{2,1,0:T(8,128)(2,1)S(1)} %get-tuple-element.53), channel_id=1, source_target_pairs={{0,2},{1,3},{2,0},{3,1},{4,6},{5,7},{6,4},{7,5},{8,10},{9,11},{10,... | collective-permute-start | bytes 589832 | tf_op jit(solution)/shard_map/out_b/ppermute | solution.py:430
  23.2 6.8 %collective-permute-start.13 = (bf16[2,192,256]{2,1,0:T(8,128)(2,1)S(1)}, bf16[2,192,256]{2,1,0:T(8,128)(2,1)S(1)}, u32[]{:S(2)}, u32[]{:S(2)}) collective-permute-start(bf16[2,192,256]{2,1,0:T(8,128)(2,1)S(1)} %get-tuple-element.71), channel_id=1, source_target_pairs={{0,1},{1,0},{2,3},{3,2},{4,5},{5,4},{6,7},{7,6},{8,9},{9,8},{10,11... | collective-permute-start | bytes 589832 | tf_op jit(solution)/shard_map/in_75/ppermute | solution.py:430
  25.7 9.1 %collective-permute-start.8 = (bf16[2,192,256]{2,1,0:T(8,128)(2,1)S(1)}, bf16[2,192,256]{2,1,0:T(8,128)(2,1)S(1)}, u32[]{:S(2)}, u32[]{:S(2)}) collective-permute-start(bf16[2,192,256]{2,1,0:T(8,128)(2,1)S(1)} %add_convert_fusion), channel_id=1, source_target_pairs={{0,4},{1,5},{2,6},{3,7},{4,0},{5,1},{6,2},{7,3},{8,12},{9,13},{10,... | collective-permute-start | bytes 589832 | tf_op jit(solution)/shard_map/out_mid/ppermute | solution.py:430
  27.9 4.6 %collective-permute-start.12 = (bf16[1,192,256]{2,1,0:T(8,128)(2,1)S(1)}, bf16[1,192,256]{2,1,0:T(8,128)(2,1)S(1)}, u32[]{:S(2)}, u32[]{:S(2)}) collective-permute-start(bf16[1,192,256]{2,1,0:T(8,128)(2,1)S(1)} %get-tuple-element.69), channel_id=1, source_target_pairs={{0,1},{1,0},{2,3},{3,2},{4,5},{5,4},{6,7},{7,6},{8,9},{9,8},{10,11... | collective-permute-start | bytes 294920 | tf_op jit(solution)/shard_map/in_3/ppermute | solution.py:430
  30.0 5.8 %collective-permute-start.14 = (bf16[1,192,256]{2,1,0:T(8,128)(2,1)S(1)}, bf16[1,192,256]{2,1,0:T(8,128)(2,1)S(1)}, u32[]{:S(2)}, u32[]{:S(2)}) collective-permute-start(bf16[1,192,256]{2,1,0:T(8,128)(2,1)S(1)} %add_convert_fusion.3), channel_id=1, source_target_pairs={{0,2},{1,3},{2,0},{3,1},{4,6},{5,7},{6,4},{7,5},{8,10},{9,11},{10,... | collective-permute-start | bytes 294920 | tf_op jit(solution)/shard_map/in_6/ppermute | solution.py:430
  32.5 8.8 %collective-permute-start.17 = (bf16[1,192,256]{2,1,0:T(8,128)(2,1)S(1)}, bf16[1,192,256]{2,1,0:T(8,128)(2,1)S(1)}, u32[]{:S(2)}, u32[]{:S(2)}) collective-permute-start(bf16[1,192,256]{2,1,0:T(8,128)(2,1)S(1)} %add_convert_fusion.4), channel_id=1, source_target_pairs={{0,2},{1,3},{2,0},{3,1},{4,6},{5,7},{6,4},{7,5},{8,10},{9,11},{10,... | collective-permute-start | bytes 294920 | tf_op jit(solution)/shard_map/in_2/ppermute | solution.py:430
  34.2 5.5 %collective-permute-start.19 = (f32[2,48,256]{2,1,0:T(8,128)S(1)}, f32[2,48,256]{2,1,0:T(8,128)S(1)}, u32[]{:S(2)}, u32[]{:S(2)}) collective-permute-start(f32[2,48,256]{2,1,0:T(8,128)S(1)} %get-tuple-element.80), channel_id=1, source_target_pairs={{0,8},{8,0},{16,24},{24,16},{1,9},{9,1},{17,25},{25,17},{2,10},{10... | collective-permute-start | bytes 294920 | tf_op jit(solution)/shard_map/grad_prefix_core/ppermute | solution.py:430
  35.8 8.0 %collective-permute-start.18 = (bf16[1,192,256]{2,1,0:T(8,128)(2,1)S(1)}, bf16[1,192,256]{2,1,0:T(8,128)(2,1)S(1)}, u32[]{:S(2)}, u32[]{:S(2)}) collective-permute-start(bf16[1,192,256]{2,1,0:T(8,128)(2,1)S(1)} %add_convert_fusion.2), channel_id=1, source_target_pairs={{0,4},{1,5},{2,6},{3,7},{4,0},{5,1},{6,2},{7,3},{8,12},{9,13},{10,... | collective-permute-start | bytes 294920 | tf_op jit(solution)/shard_map/in_4/ppermute | solution.py:430
  37.6 6.3 %collective-permute-start.15 = (bf16[1,192,256]{2,1,0:T(8,128)(2,1)S(1)}, bf16[1,192,256]{2,1,0:T(8,128)(2,1)S(1)}, u32[]{:S(2)}, u32[]{:S(2)}) collective-permute-start(bf16[1,192,256]{2,1,0:T(8,128)(2,1)S(1)} %add_convert_fusion.1), channel_id=1, source_target_pairs={{0,1},{1,0},{2,3},{3,2},{4,5},{5,4},{6,7},{7,6},{8,9},{9,8},{10,11... | collective-permute-start | bytes 294920 | tf_op jit(solution)/shard_map/out_x/ppermute | solution.py:430
  39.1 4.7 %collective-permute-start.16 = (bf16[1,192,256]{2,1,0:T(8,128)(2,1)S(1)}, bf16[1,192,256]{2,1,0:T(8,128)(2,1)S(1)}, u32[]{:S(2)}, u32[]{:S(2)}) collective-permute-start(bf16[1,192,256]{2,1,0:T(8,128)(2,1)S(1)} %get-tuple-element.77), channel_id=1, source_target_pairs={{0,1},{1,0},{2,3},{3,2},{4,5},{5,4},{6,7},{7,6},{8,9},{9,8},{10,11... | collective-permute-start | bytes 294920 | tf_op jit(solution)/shard_map/in_1/ppermute | solution.py:430
  39.7 4.2 %collective-permute-start.20 = (f32[1,48,256]{2,1,0:T(8,128)S(1)}, f32[1,48,256]{2,1,0:T(8,128)S(1)}, u32[]{:S(2)}, u32[]{:S(2)}) collective-permute-start(f32[1,48,256]{2,1,0:T(8,128)S(1)} %slice_add_fusion), channel_id=1, source_target_pairs={{0,16},{8,24},{16,0},{24,8},{1,17},{9,25},{17,1},{25,9},{2,18},{10... | collective-permute-start | bytes 147464 | tf_op jit(solution)/shard_map/grad_prefix_y/ppermute | solution.py:430
where the time goes:
time: 44.8 us; the launch traced here: 44.7 us
  starting transfers between devices  28.3 us (63%)
  waiting for transfers between devices  8.73 us (19%)
  Pallas kernels  6.69 us (15%)
  between operations  0.71 us (2%)
    ppermute x21, starting transfers between devices, trade(): lax.ppermute(block, axis, [(i, i ^ step) for i in range(lax.axis_size(axi...  28.3 us
    ppermute x21, waiting for transfers between devices, trade(): lax.ppermute(block, axis, [(i, i ^ step) for i in range(lax.axis_size(axi...  8.73 us
    pallas_call x1, Pallas kernels, project(): pl.pallas_call(project_kernel, in_specs=[HBM] * len(operands), out_specs=...  2.63 us
    pallas_call x1, Pallas kernels, backward(): pl.pallas_call(functools.partial(backward_kernel, slots, names), in_specs...  2.32 us
    pallas_call x1, Pallas kernels, forward(): pl.pallas_call(functools.partial(forward_kernel, slots, names), in_specs=...  0.97 us
  transfers between devices with their start and end apart: 21, of which 9 were waited for; matrix products, arithmetic and copies ran while one was open for 0% of the time, Pallas kernels for 13%

commit v1 on v0

--- a/solution.py
+++ b/solution.py
@@ -12,7 +12,7 @@
 ROWS = 16
 HELD = ((0,), (4, 2), (6,), (1,), (5, 3), (7,))
 OUT = ((6, 7), (2, 3), (4, 5), (0, 1))
-TERMS = ((1, 3), (0, 2))
+TERMS = ((2, 3), (0, 1))
 IN = ((7, 5), (3,), (1,), (6,), (4,), (2,), (0,))
 F32 = jnp.float32
 BF16 = jnp.bfloat16
@@ -496,8 +496,8 @@
     in_2 = total(in_2, got_3)
     got_2 = trade("in_2", in_2, "mp", 2)
     if chips == 4:
-        got = trade("grad_prefix_core", after(terms[0], in_2), "dp", 1)
-        last = trade("grad_prefix_y", terms[1][1:] + got[1:], "dp", 2)
+        got = trade("grad_prefix_y", after(terms[0], in_2), "dp", 2)
+        last = trade("grad_prefix_core", terms[1][1:] + got[1:], "dp", 1)
     in_4 = total(after(in_4, got_b, got_out, in_2), got_75[1:], got_6)
     got_4 = trade("in_4", in_4, "mp", 4)
     got_1 = trade("in_1", after(in_1, in_4), "mp", 1)

time: 44.8 us -> 45.2 us (level)
  no operation moved by 1% of the time
where the time goes in v1:
time: 45.2 us; the launch traced here: 45 us
  starting transfers between devices  28.3 us (63%)
  waiting for transfers between devices  9.08 us (20%)
  Pallas kernels  6.69 us (15%)
  between operations  0.72 us (2%)
    ppermute x21, starting transfers between devices, trade(): lax.ppermute(block, axis, [(i, i ^ step) for i in range(lax.axis_size(axi...  28.3 us
    ppermute x21, waiting for transfers between devices, trade(): lax.ppermute(block, axis, [(i, i ^ step) for i in range(lax.axis_size(axi...  9.08 us
    pallas_call x1, Pallas kernels, project(): pl.pallas_call(project_kernel, in_specs=[HBM] * len(operands), out_specs=...  2.63 us
    pallas_call x1, Pallas kernels, backward(): pl.pallas_call(functools.partial(backward_kernel, slots, names), in_specs...  2.32 us
    pallas_call x1, Pallas kernels, forward(): pl.pallas_call(functools.partial(forward_kernel, slots, names), in_specs=...  0.97 us
  transfers between devices with their start and end apart: 21, of which 9 were waited for; matrix products, arithmetic and copies ran while one was open for 0% of the time, Pallas kernels for 13%

profile of v1, /device:TPU:0, one launch (start us, length us, event | category | flops | bytes accessed | tf_op | source)
XLA Modules:
  0.0 45.0 jit_solution(7732108324902000948)
XLA Ops:
  0.6 4.1 %collective-permute-start = (bf16[1,192,256]{2,1,0:T(8,128)(2,1)}, bf16[1,192,256]{2,1,0:T(8,128)(2,1)S(1)}, u32[]{:S(2)}, u32[]{:S(2)}) collective-permute-start(bf16[1,192,256]{2,1,0:T(8,128)(2,1)} %bitcast.3), channel_id=1, source_target_pairs={{0,4},{1,5},{2,6},{3,7},{4,0},{5,1},{6,2},{7,3},{8,12},{9,13},{10,... | collective-permute-start | bytes 294920 | tf_op jit(solution)/shard_map/gather_far/ppermute | solution.py:430
  4.7 1.5 %collective-permute-start.2 = (bf16[48,256]{1,0:T(8,128)(2,1)}, bf16[48,256]{1,0:T(8,128)(2,1)S(1)}, u32[]{:S(2)}, u32[]{:S(2)}) collective-permute-start(bf16[48,256]{1,0:T(8,128)(2,1)} %refs_9_.1), channel_id=1, source_target_pairs={{0,16},{8,24},{16,0},{24,8},{1,17},{9,25},{17,1},{25,9},{2,18},{10... | collective-permute-start | bytes 73736 | tf_op jit(solution)/shard_map/gather_prefix/ppermute | solution.py:430
  6.6 1.6 %collective-permute-start.4 = (bf16[1,192,256]{2,1,0:T(8,128)(2,1)}, bf16[1,192,256]{2,1,0:T(8,128)(2,1)S(1)}, u32[]{:S(2)}, u32[]{:S(2)}) collective-permute-start(bf16[1,192,256]{2,1,0:T(8,128)(2,1)} %bitcast.4), channel_id=1, source_target_pairs={{0,2},{1,3},{2,0},{3,1},{4,6},{5,7},{6,4},{7,5},{8,10},{9,11},{10,... | collective-permute-start | bytes 294920 | tf_op jit(solution)/shard_map/gather_near/ppermute | solution.py:430
  8.2 1.5 %collective-permute-start.10 = (bf16[1,192,256]{2,1,0:T(8,128)(2,1)}, bf16[1,192,256]{2,1,0:T(8,128)(2,1)S(1)}, u32[]{:S(2)}, u32[]{:S(2)}) collective-permute-start(bf16[1,192,256]{2,1,0:T(8,128)(2,1)} %bitcast.5), channel_id=1, source_target_pairs={{0,1},{1,0},{2,3},{3,2},{4,5},{5,4},{6,7},{7,6},{8,9},{9,8},{10,11... | collective-permute-start | bytes 294920 | tf_op jit(solution)/shard_map/gather_own_x/ppermute | solution.py:430
  9.9 1.4 %collective-permute-start.9 = (bf16[1,192,256]{2,1,0:T(8,128)(2,1)S(1)}, bf16[1,192,256]{2,1,0:T(8,128)(2,1)S(1)}, u32[]{:S(2)}, u32[]{:S(2)}) collective-permute-start(bf16[1,192,256]{2,1,0:T(8,128)(2,1)S(1)} %collective-permute-done), channel_id=1, source_target_pairs={{0,2},{1,3},{2,0},{3,1},{4,6},{5,7},{6,4},{7,5},{8,10},{9,11},{10,... | collective-permute-start | bytes 294920 | tf_op jit(solution)/shard_map/gather_both/ppermute | solution.py:430
  12.0 1.6 %collective-permute-start.5 = (bf16[2,192,256]{2,1,0:T(8,128)(2,1)S(1)}, bf16[2,192,256]{2,1,0:T(8,128)(2,1)S(1)}, u32[]{:S(2)}, u32[]{:S(2)}) collective-permute-start(bf16[2,192,256]{2,1,0:T(8,128)(2,1)S(1)} %constant_dynamic-update-slice_fusion.refs_4_), channel_id=1, source_target_pairs={{0,1},{1,0},{2,3},{3,2},{4,5},{5,4},{6,7},{7,6},{8,9},{9,8},{10,11... | collective-permute-start | bytes 589832 | tf_op jit(solution)/shard_map/gather_pair_x/ppermute | solution.py:430
  13.6 2.6 %shard_map.139 = (s32[4]{0:T(128)S(4)}, s32[2]{0:T(128)S(4)}, s32[2]{0:T(128)S(4)}, bf16[192,256]{1,0:T(8,128)(2,1)S(1)}, bf16[192,128]{1,0:T(8,128)(2,1)S(1)}, ...) custom-call(s32[4]{0:T(128)} %refs_0_.1, ...), custom_call_target="tpu_custom_call" | custom-call | flops 2990000128 | tf_op jit(solution)/shard_map/pallas_call | solution.py:173
  16.8 1.0 %shard_map.140 = (bf16[2,1,192,80]{3,2,1,0:T(8,128)(2,1)S(1)}, bf16[2,1,192,96]{3,2,1,0:T(8,128)(2,1)S(1)}, f32[192,256]{1,0:T(8,128)S(1)}, bf16[192,256]{1,0:T(...) custom-call(s32[4]{0:T(128)S(4)} %get-tuple-element.44.refs_0_, ...), custom_call_target="tpu_custom_call" | custom-call | flops 1955000064 | tf_op jit(solution)/shard_map/pallas_call | solution.py:286
  17.7 1.5 %collective-permute-start.7 = (bf16[2,192,256]{2,1,0:T(8,128)(2,1)S(1)}, bf16[2,192,256]{2,1,0:T(8,128)(2,1)S(1)}, u32[]{:S(2)}, u32[]{:S(2)}) collective-permute-start(bf16[2,192,256]{2,1,0:T(8,128)(2,1)S(1)} %get-tuple-element.55), channel_id=1, source_target_pairs={{0,2},{1,3},{2,0},{3,1},{4,6},{5,7},{6,4},{7,5},{8,10},{9,11},{10,... | collective-permute-start | bytes 589832 | tf_op jit(solution)/shard_map/out_a/ppermute | solution.py:430
  19.9 1.0 %collective-permute-done.11.refs_8_ = bf16[1,192,256]{2,1,0:T(8,128)(2,1)S(1)} collective-permute-done((bf16[1,192,256]{2,1,0:T(8,128)(2,1)S(1)}, bf16[1,192,256]{2,1,0:T(8,128)(2,1)S(1)}, u32[]{:S(2)}, u32[]{:S(2)}) %collective-permute-start.11) | collective-permute-done | bytes 98336 | tf_op jit(solution)/shard_map/gather_both_x/ppermute | solution.py:430
  20.9 2.3 %shard_map.141 = (f32[2,48,256]{2,1,0:T(8,128)S(1)}, f32[2,48,256]{2,1,0:T(8,128)S(1)}, bf16[2,192,256]{2,1,0:T(8,128)(2,1)S(1)}, bf16[1,192,256]{2,1,0:T(8,128)...) custom-call(s32[4]{0:T(128)S(4)} %get-tuple-element.44.refs_0_, ...), custom_call_target="tpu_custom_call" | custom-call | flops 4024999936 | tf_op jit(solution)/shard_map/pallas_call | solution.py:382
  23.2 1.4 %collective-permute-start.13 = (bf16[2,192,256]{2,1,0:T(8,128)(2,1)S(1)}, bf16[2,192,256]{2,1,0:T(8,128)(2,1)S(1)}, u32[]{:S(2)}, u32[]{:S(2)}) collective-permute-start(bf16[2,192,256]{2,1,0:T(8,128)(2,1)S(1)} %get-tuple-element.71), channel_id=1, source_target_pairs={{0,1},{1,0},{2,3},{3,2},{4,5},{5,4},{6,7},{7,6},{8,9},{9,8},{10,11... | collective-permute-start | bytes 589832 | tf_op jit(solution)/shard_map/in_75/ppermute | solution.py:430
  24.7 1.0 %collective-permute-done.7 = bf16[2,192,256]{2,1,0:T(8,128)(2,1)S(1)} collective-permute-done((bf16[2,192,256]{2,1,0:T(8,128)(2,1)S(1)}, bf16[2,192,256]{2,1,0:T(8,128)(2,1)S(1)}, u32[]{:S(2)}, u32[]{:S(2)}) %collective-permute-start.7) | collective-permute-done | bytes 196640 | tf_op jit(solution)/shard_map/out_a/ppermute | solution.py:430
  25.7 2.2 %collective-permute-start.8 = (bf16[2,192,256]{2,1,0:T(8,128)(2,1)S(1)}, bf16[2,192,256]{2,1,0:T(8,128)(2,1)S(1)}, u32[]{:S(2)}, u32[]{:S(2)}) collective-permute-start(bf16[2,192,256]{2,1,0:T(8,128)(2,1)S(1)} %add_convert_fusion), channel_id=1, source_target_pairs={{0,4},{1,5},{2,6},{3,7},{4,0},{5,1},{6,2},{7,3},{8,12},{9,13},{10,... | collective-permute-start | bytes 589832 | tf_op jit(solution)/shard_map/out_mid/ppermute | solution.py:430
  27.9 1.5 %collective-permute-start.12 = (bf16[1,192,256]{2,1,0:T(8,128)(2,1)S(1)}, bf16[1,192,256]{2,1,0:T(8,128)(2,1)S(1)}, u32[]{:S(2)}, u32[]{:S(2)}) collective-permute-start(bf16[1,192,256]{2,1,0:T(8,128)(2,1)S(1)} %get-tuple-element.69), channel_id=1, source_target_pairs={{0,1},{1,0},{2,3},{3,2},{4,5},{5,4},{6,7},{7,6},{8,9},{9,8},{10,11... | collective-permute-start | bytes 294920 | tf_op jit(solution)/shard_map/in_3/ppermute | solution.py:430
  30.0 1.3 %collective-permute-start.14 = (bf16[1,192,256]{2,1,0:T(8,128)(2,1)S(1)}, bf16[1,192,256]{2,1,0:T(8,128)(2,1)S(1)}, u32[]{:S(2)}, u32[]{:S(2)}) collective-permute-start(bf16[1,192,256]{2,1,0:T(8,128)(2,1)S(1)} %add_convert_fusion.3), channel_id=1, source_target_pairs={{0,2},{1,3},{2,0},{3,1},{4,6},{5,7},{6,4},{7,5},{8,10},{9,11},{10,... | collective-permute-start | bytes 294920 | tf_op jit(solution)/shard_map/in_6/ppermute | solution.py:430
  31.3 1.2 %collective-permute-done.12 = bf16[1,192,256]{2,1,0:T(8,128)(2,1)S(1)} collective-permute-done((bf16[1,192,256]{2,1,0:T(8,128)(2,1)S(1)}, bf16[1,192,256]{2,1,0:T(8,128)(2,1)S(1)}, u32[]{:S(2)}, u32[]{:S(2)}) %collective-permute-start.12) | collective-permute-done | bytes 98336 | tf_op jit(solution)/shard_map/in_3/ppermute | solution.py:430
  32.5 1.7 %collective-permute-start.17 = (bf16[1,192,256]{2,1,0:T(8,128)(2,1)S(1)}, bf16[1,192,256]{2,1,0:T(8,128)(2,1)S(1)}, u32[]{:S(2)}, u32[]{:S(2)}) collective-permute-start(bf16[1,192,256]{2,1,0:T(8,128)(2,1)S(1)} %add_convert_fusion.4), channel_id=1, source_target_pairs={{0,2},{1,3},{2,0},{3,1},{4,6},{5,7},{6,4},{7,5},{8,10},{9,11},{10,... | collective-permute-start | bytes 294920 | tf_op jit(solution)/shard_map/in_2/ppermute | solution.py:430
  34.2 1.5 %collective-permute-start.19 = (f32[2,48,256]{2,1,0:T(8,128)S(1)}, f32[2,48,256]{2,1,0:T(8,128)S(1)}, u32[]{:S(2)}, u32[]{:S(2)}) collective-permute-start(f32[2,48,256]{2,1,0:T(8,128)S(1)} %get-tuple-element.80), channel_id=1, source_target_pairs={{0,16},{8,24},{16,0},{24,8},{1,17},{9,25},{17,1},{25,9},{2,18},{10... | collective-permute-start | bytes 294920 | tf_op jit(solution)/shard_map/grad_prefix_y/ppermute | solution.py:430
  35.8 1.7 %collective-permute-start.18 = (bf16[1,192,256]{2,1,0:T(8,128)(2,1)S(1)}, bf16[1,192,256]{2,1,0:T(8,128)(2,1)S(1)}, u32[]{:S(2)}, u32[]{:S(2)}) collective-permute-start(bf16[1,192,256]{2,1,0:T(8,128)(2,1)S(1)} %add_convert_fusion.2), channel_id=1, source_target_pairs={{0,4},{1,5},{2,6},{3,7},{4,0},{5,1},{6,2},{7,3},{8,12},{9,13},{10,... | collective-permute-start | bytes 294920 | tf_op jit(solution)/shard_map/in_4/ppermute | solution.py:430
  37.6 2.0 %collective-permute-start.15 = (bf16[1,192,256]{2,1,0:T(8,128)(2,1)S(1)}, bf16[1,192,256]{2,1,0:T(8,128)(2,1)S(1)}, u32[]{:S(2)}, u32[]{:S(2)}) collective-permute-start(bf16[1,192,256]{2,1,0:T(8,128)(2,1)S(1)} %add_convert_fusion.1), channel_id=1, source_target_pairs={{0,1},{1,0},{2,3},{3,2},{4,5},{5,4},{6,7},{7,6},{8,9},{9,8},{10,11... | collective-permute-start | bytes 294920 | tf_op jit(solution)/shard_map/out_x/ppermute | solution.py:430
  39.8 1.2 %collective-permute-done.20.refs_10_ = f32[1,48,256]{2,1,0:T(8,128)S(1)} collective-permute-done((f32[1,48,256]{2,1,0:T(8,128)S(1)}, f32[1,48,256]{2,1,0:T(8,128)S(1)}, u32[]{:S(2)}, u32[]{:S(2)}) %collective-permute-start.20) | collective-permute-done | bytes 49184 | tf_op jit(solution)/shard_map/grad_prefix_core/ppermute | solution.py:430
  41.0 1.3 %collective-permute-done.15.refs_3_ = bf16[1,192,256]{2,1,0:T(8,128)(2,1)S(1)} collective-permute-done((bf16[1,192,256]{2,1,0:T(8,128)(2,1)S(1)}, bf16[1,192,256]{2,1,0:T(8,128)(2,1)S(1)}, u32[]{:S(2)}, u32[]{:S(2)}) %collective-permute-start.15) | collective-permute-done | bytes 98336 | tf_op jit(solution)/shard_map/out_x/ppermute | solution.py:430
  42.3 1.9 %collective-permute-done.16.refs_5_ = bf16[1,192,256]{2,1,0:T(8,128)(2,1)S(1)} collective-permute-done((bf16[1,192,256]{2,1,0:T(8,128)(2,1)S(1)}, bf16[1,192,256]{2,1,0:T(8,128)(2,1)S(1)}, u32[]{:S(2)}, u32[]{:S(2)}) %collective-permute-start.16) | collective-permute-done | bytes 98336 | tf_op jit(solution)/shard_map/in_1/ppermute | solution.py:430
  (32 shorter events, 4.3 us)
Async XLA Ops:
  0.6 9.2 %collective-permute-start = (bf16[1,192,256]{2,1,0:T(8,128)(2,1)}, bf16[1,192,256]{2,1,0:T(8,128)(2,1)S(1)}, u32[]{:S(2)}, u32[]{:S(2)}) collective-permute-start(bf16[1,192,256]{2,1,0:T(8,128)(2,1)} %bitcast.3), channel_id=1, source_target_pairs={{0,4},{1,5},{2,6},{3,7},{4,0},{5,1},{6,2},{7,3},{8,12},{9,13},{10,... | collective-permute-start | bytes 294920 | tf_op jit(solution)/shard_map/gather_far/ppermute | solution.py:430
  4.7 3.4 %collective-permute-start.1 = (bf16[48,256]{1,0:T(8,128)(2,1)}, bf16[48,256]{1,0:T(8,128)(2,1)S(1)}, u32[]{:S(2)}, u32[]{:S(2)}) collective-permute-start(bf16[48,256]{1,0:T(8,128)(2,1)} %refs_9_.1), channel_id=1, source_target_pairs={{0,8},{8,0},{16,24},{24,16},{1,9},{9,1},{17,25},{25,17},{2,10},{10... | collective-permute-start | bytes 73736 | tf_op jit(solution)/shard_map/gather_prefix/ppermute | solution.py:430
  4.7 4.9 %collective-permute-start.2 = (bf16[48,256]{1,0:T(8,128)(2,1)}, bf16[48,256]{1,0:T(8,128)(2,1)S(1)}, u32[]{:S(2)}, u32[]{:S(2)}) collective-permute-start(bf16[48,256]{1,0:T(8,128)(2,1)} %refs_9_.1), channel_id=1, source_target_pairs={{0,16},{8,24},{16,0},{24,8},{1,17},{9,25},{17,1},{25,9},{2,18},{10... | collective-permute-start | bytes 73736 | tf_op jit(solution)/shard_map/gather_prefix/ppermute | solution.py:430
  6.3 3.5 %collective-permute-start.3 = (bf16[48,256]{1,0:T(8,128)(2,1)}, bf16[48,256]{1,0:T(8,128)(2,1)S(1)}, u32[]{:S(2)}, u32[]{:S(2)}) collective-permute-start(bf16[48,256]{1,0:T(8,128)(2,1)} %refs_9_.1), channel_id=1, source_target_pairs={{0,24},{8,16},{16,8},{24,0},{1,25},{9,17},{17,9},{25,1},{2,26},{10... | collective-permute-start | bytes 73736 | tf_op jit(solution)/shard_map/gather_prefix/ppermute | solution.py:430
  6.6 5.4 %collective-permute-start.4 = (bf16[1,192,256]{2,1,0:T(8,128)(2,1)}, bf16[1,192,256]{2,1,0:T(8,128)(2,1)S(1)}, u32[]{:S(2)}, u32[]{:S(2)}) collective-permute-start(bf16[1,192,256]{2,1,0:T(8,128)(2,1)} %bitcast.4), channel_id=1, source_target_pairs={{0,2},{1,3},{2,0},{3,1},{4,6},{5,7},{6,4},{7,5},{8,10},{9,11},{10,... | collective-permute-start | bytes 294920 | tf_op jit(solution)/shard_map/gather_near/ppermute | solution.py:430
  8.2 11.8 %collective-permute-start.10 = (bf16[1,192,256]{2,1,0:T(8,128)(2,1)}, bf16[1,192,256]{2,1,0:T(8,128)(2,1)S(1)}, u32[]{:S(2)}, u32[]{:S(2)}) collective-permute-start(bf16[1,192,256]{2,1,0:T(8,128)(2,1)} %bitcast.5), channel_id=1, source_target_pairs={{0,1},{1,0},{2,3},{3,2},{4,5},{5,4},{6,7},{7,6},{8,9},{9,8},{10,11... | collective-permute-start | bytes 294920 | tf_op jit(solution)/shard_map/gather_own_x/ppermute | solution.py:430
  9.9 6.3 %collective-permute-start.9 = (bf16[1,192,256]{2,1,0:T(8,128)(2,1)S(1)}, bf16[1,192,256]{2,1,0:T(8,128)(2,1)S(1)}, u32[]{:S(2)}, u32[]{:S(2)}) collective-permute-start(bf16[1,192,256]{2,1,0:T(8,128)(2,1)S(1)} %collective-permute-done), channel_id=1, source_target_pairs={{0,2},{1,3},{2,0},{3,1},{4,6},{5,7},{6,4},{7,5},{8,10},{9,11},{10,... | collective-permute-start | bytes 294920 | tf_op jit(solution)/shard_map/gather_both/ppermute | solution.py:430
  12.0 7.3 %collective-permute-start.5 = (bf16[2,192,256]{2,1,0:T(8,128)(2,1)S(1)}, bf16[2,192,256]{2,1,0:T(8,128)(2,1)S(1)}, u32[]{:S(2)}, u32[]{:S(2)}) collective-permute-start(bf16[2,192,256]{2,1,0:T(8,128)(2,1)S(1)} %constant_dynamic-update-slice_fusion.refs_4_), channel_id=1, source_target_pairs={{0,1},{1,0},{2,3},{3,2},{4,5},{5,4},{6,7},{7,6},{8,9},{9,8},{10,11... | collective-permute-start | bytes 589832 | tf_op jit(solution)/shard_map/gather_pair_x/ppermute | solution.py:430
  13.6 3.2 %copy-start = (bf16[256,2048]{1,0:T(8,128)(2,1)S(1)}, bf16[256,2048]{1,0:T(8,128)(2,1)}, u32[]{:S(2)}) copy-start(bf16[256,2048]{1,0:T(8,128)(2,1)} %refs_17_.1) | copy-start | bytes 3145732
  16.2 4.7 %collective-permute-start.11 = (bf16[1,192,256]{2,1,0:T(8,128)(2,1)S(1)}, bf16[1,192,256]{2,1,0:T(8,128)(2,1)S(1)}, u32[]{:S(2)}, u32[]{:S(2)}) collective-permute-start(bf16[1,192,256]{2,1,0:T(8,128)(2,1)S(1)} %collective-permute-done.9.refs_5_), channel_id=1, source_target_pairs={{0,1},{1,0},{2,3},{3,2},{4,5},{5,4},{6,7},{7,6},{8,9},{9,8},{10,11... | collective-permute-start | bytes 294920 | tf_op jit(solution)/shard_map/gather_both_x/ppermute | solution.py:430
  17.7 7.9 %collective-permute-start.7 = (bf16[2,192,256]{2,1,0:T(8,128)(2,1)S(1)}, bf16[2,192,256]{2,1,0:T(8,128)(2,1)S(1)}, u32[]{:S(2)}, u32[]{:S(2)}) collective-permute-start(bf16[2,192,256]{2,1,0:T(8,128)(2,1)S(1)} %get-tuple-element.55), channel_id=1, source_target_pairs={{0,2},{1,3},{2,0},{3,1},{4,6},{5,7},{6,4},{7,5},{8,10},{9,11},{10,... | collective-permute-start | bytes 589832 | tf_op jit(solution)/shard_map/out_a/ppermute | solution.py:430
  19.2 16.5 %collective-permute-start.6 = (bf16[2,192,256]{2,1,0:T(8,128)(2,1)S(1)}, bf16[2,192,256]{2,1,0:T(8,128)(2,1)S(1)}, u32[]{:S(2)}, u32[]{:S(2)}) collective-permute-start(bf16[2,192,256]{2,1,0:T(8,128)(2,1)S(1)} %get-tuple-element.53), channel_id=1, source_target_pairs={{0,2},{1,3},{2,0},{3,1},{4,6},{5,7},{6,4},{7,5},{8,10},{9,11},{10,... | collective-permute-start | bytes 589832 | tf_op jit(solution)/shard_map/out_b/ppermute | solution.py:430
  23.2 6.8 %collective-permute-start.13 = (bf16[2,192,256]{2,1,0:T(8,128)(2,1)S(1)}, bf16[2,192,256]{2,1,0:T(8,128)(2,1)S(1)}, u32[]{:S(2)}, u32[]{:S(2)}) collective-permute-start(bf16[2,192,256]{2,1,0:T(8,128)(2,1)S(1)} %get-tuple-element.71), channel_id=1, source_target_pairs={{0,1},{1,0},{2,3},{3,2},{4,5},{5,4},{6,7},{7,6},{8,9},{9,8},{10,11... | collective-permute-start | bytes 589832 | tf_op jit(solution)/shard_map/in_75/ppermute | solution.py:430
  25.7 10.0 %collective-permute-start.8 = (bf16[2,192,256]{2,1,0:T(8,128)(2,1)S(1)}, bf16[2,192,256]{2,1,0:T(8,128)(2,1)S(1)}, u32[]{:S(2)}, u32[]{:S(2)}) collective-permute-start(bf16[2,192,256]{2,1,0:T(8,128)(2,1)S(1)} %add_convert_fusion), channel_id=1, source_target_pairs={{0,4},{1,5},{2,6},{3,7},{4,0},{5,1},{6,2},{7,3},{8,12},{9,13},{10,... | collective-permute-start | bytes 589832 | tf_op jit(solution)/shard_map/out_mid/ppermute | solution.py:430
  27.9 4.6 %collective-permute-start.12 = (bf16[1,192,256]{2,1,0:T(8,128)(2,1)S(1)}, bf16[1,192,256]{2,1,0:T(8,128)(2,1)S(1)}, u32[]{:S(2)}, u32[]{:S(2)}) collective-permute-start(bf16[1,192,256]{2,1,0:T(8,128)(2,1)S(1)} %get-tuple-element.69), channel_id=1, source_target_pairs={{0,1},{1,0},{2,3},{3,2},{4,5},{5,4},{6,7},{7,6},{8,9},{9,8},{10,11... | collective-permute-start | bytes 294920 | tf_op jit(solution)/shard_map/in_3/ppermute | solution.py:430
  30.0 5.8 %collective-permute-start.14 = (bf16[1,192,256]{2,1,0:T(8,128)(2,1)S(1)}, bf16[1,192,256]{2,1,0:T(8,128)(2,1)S(1)}, u32[]{:S(2)}, u32[]{:S(2)}) collective-permute-start(bf16[1,192,256]{2,1,0:T(8,128)(2,1)S(1)} %add_convert_fusion.3), channel_id=1, source_target_pairs={{0,2},{1,3},{2,0},{3,1},{4,6},{5,7},{6,4},{7,5},{8,10},{9,11},{10,... | collective-permute-start | bytes 294920 | tf_op jit(solution)/shard_map/in_6/ppermute | solution.py:430
  32.5 7.3 %collective-permute-start.17 = (bf16[1,192,256]{2,1,0:T(8,128)(2,1)S(1)}, bf16[1,192,256]{2,1,0:T(8,128)(2,1)S(1)}, u32[]{:S(2)}, u32[]{:S(2)}) collective-permute-start(bf16[1,192,256]{2,1,0:T(8,128)(2,1)S(1)} %add_convert_fusion.4), channel_id=1, source_target_pairs={{0,2},{1,3},{2,0},{3,1},{4,6},{5,7},{6,4},{7,5},{8,10},{9,11},{10,... | collective-permute-start | bytes 294920 | tf_op jit(solution)/shard_map/in_2/ppermute | solution.py:430
  34.2 5.5 %collective-permute-start.19 = (f32[2,48,256]{2,1,0:T(8,128)S(1)}, f32[2,48,256]{2,1,0:T(8,128)S(1)}, u32[]{:S(2)}, u32[]{:S(2)}) collective-permute-start(f32[2,48,256]{2,1,0:T(8,128)S(1)} %get-tuple-element.80), channel_id=1, source_target_pairs={{0,16},{8,24},{16,0},{24,8},{1,17},{9,25},{17,1},{25,9},{2,18},{10... | collective-permute-start | bytes 294920 | tf_op jit(solution)/shard_map/grad_prefix_y/ppermute | solution.py:430
  35.8 8.4 %collective-permute-start.18 = (bf16[1,192,256]{2,1,0:T(8,128)(2,1)S(1)}, bf16[1,192,256]{2,1,0:T(8,128)(2,1)S(1)}, u32[]{:S(2)}, u32[]{:S(2)}) collective-permute-start(bf16[1,192,256]{2,1,0:T(8,128)(2,1)S(1)} %add_convert_fusion.2), channel_id=1, source_target_pairs={{0,4},{1,5},{2,6},{3,7},{4,0},{5,1},{6,2},{7,3},{8,12},{9,13},{10,... | collective-permute-start | bytes 294920 | tf_op jit(solution)/shard_map/in_4/ppermute | solution.py:430
  37.6 4.7 %collective-permute-start.15 = (bf16[1,192,256]{2,1,0:T(8,128)(2,1)S(1)}, bf16[1,192,256]{2,1,0:T(8,128)(2,1)S(1)}, u32[]{:S(2)}, u32[]{:S(2)}) collective-permute-start(bf16[1,192,256]{2,1,0:T(8,128)(2,1)S(1)} %add_convert_fusion.1), channel_id=1, source_target_pairs={{0,1},{1,0},{2,3},{3,2},{4,5},{5,4},{6,7},{7,6},{8,9},{9,8},{10,11... | collective-permute-start | bytes 294920 | tf_op jit(solution)/shard_map/out_x/ppermute | solution.py:430
  39.6 4.6 %collective-permute-start.16 = (bf16[1,192,256]{2,1,0:T(8,128)(2,1)S(1)}, bf16[1,192,256]{2,1,0:T(8,128)(2,1)S(1)}, u32[]{:S(2)}, u32[]{:S(2)}) collective-permute-start(bf16[1,192,256]{2,1,0:T(8,128)(2,1)S(1)} %get-tuple-element.77), channel_id=1, source_target_pairs={{0,1},{1,0},{2,3},{3,2},{4,5},{5,4},{6,7},{7,6},{8,9},{9,8},{10,11... | collective-permute-start | bytes 294920 | tf_op jit(solution)/shard_map/in_1/ppermute | solution.py:430
  39.7 1.3 %collective-permute-start.20 = (f32[1,48,256]{2,1,0:T(8,128)S(1)}, f32[1,48,256]{2,1,0:T(8,128)S(1)}, u32[]{:S(2)}, u32[]{:S(2)}) collective-permute-start(f32[1,48,256]{2,1,0:T(8,128)S(1)} %slice_add_fusion), channel_id=1, source_target_pairs={{0,8},{8,0},{16,24},{24,16},{1,9},{9,1},{17,25},{25,17},{2,10},{10... | collective-permute-start | bytes 147464 | tf_op jit(solution)/shard_map/grad_prefix_core/ppermute | solution.py:430

commit v2 on v1

--- a/solution.py
+++ b/solution.py
@@ -122,7 +122,7 @@
 
     copies = Copies(sems)
     depth = hidden.shape[1]
-    steps = 4
+    steps = 8
     part = depth // steps
     places, end = [], 0
     for w in (w_q, w_k, w_v):
@@ -175,7 +175,7 @@
         in_specs=[HBM] * len(operands),
         out_specs=[SMEM] * 3 + [VMEM] * len(kept),
         out_shape=[pltpu.SMEM(x.shape, jnp.int32) for x in scalars] + in_vmem(kept),
-        scratch_shapes=[pltpu.VMEM(hidden.shape, hidden.dtype), pltpu.SemaphoreType.DMA((32,))],
+        scratch_shapes=[pltpu.VMEM(hidden.shape, hidden.dtype), pltpu.SemaphoreType.DMA((48,))],
         compiler_params=pltpu.CompilerParams(vmem_limit_bytes=vmem_room(prefix.shape[0])),
         cost_estimate=lasting(2.6),
     )(*held_in(pltpu.HBM, operands))
@@ -500,7 +500,7 @@
         last = trade("grad_prefix_core", terms[1][1:] + got[1:], "dp", 1)
     in_4 = total(after(in_4, got_b, got_out, in_2), got_75[1:], got_6)
     got_4 = trade("in_4", in_4, "mp", 4)
-    got_1 = trade("in_1", after(in_1, in_4), "mp", 1)
+    got_1 = trade("in_1", after(in_1, in_2), "mp", 1)
     got_x = trade("out_x", total(after(kept_b, in_4)[1:], got_b[1:], got_out[1:]), "mp", 1)
     groups = [
         [(kept_b, 0), (got_b, 0), (got_out, 0), (got_x, 0)],

time: 45.2 us -> 45.3 us (level)
  transfers between devices with their start and end apart: 21 -> 21, of which waited for: 9 -> 10; matrix products, arithmetic and copies ran while one was open for 0% -> 0% of each run, Pallas kernels for 13% -> 13%
where the time goes in v2:
time: 45.3 us; the launch traced here: 45.2 us
  starting transfers between devices  28 us (62%)
  waiting for transfers between devices  9.37 us (21%)
  Pallas kernels  6.79 us (15%)
  between operations  0.74 us (2%)
    ppermute x21, starting transfers between devices, trade(): lax.ppermute(block, axis, [(i, i ^ step) for i in range(lax.axis_size(axi...  28 us
    ppermute x21, waiting for transfers between devices, trade(): lax.ppermute(block, axis, [(i, i ^ step) for i in range(lax.axis_size(axi...  9.37 us
    pallas_call x1, Pallas kernels, project(): pl.pallas_call(project_kernel, in_specs=[HBM] * len(operands), out_specs=...  2.73 us
    pallas_call x1, Pallas kernels, backward(): pl.pallas_call(functools.partial(backward_kernel, slots, names), in_specs...  2.32 us
    pallas_call x1, Pallas kernels, forward(): pl.pallas_call(functools.partial(forward_kernel, slots, names), in_specs=...  0.98 us
  transfers between devices with their start and end apart: 21, of which 10 were waited for; matrix products, arithmetic and copies ran while one was open for 0% of the time, Pallas kernels for 13%

profile of v2, /device:TPU:0, one launch (start us, length us, event | category | flops | bytes accessed | tf_op | source)
XLA Modules:
  0.0 45.2 jit_solution(5897166005179365507)
XLA Ops:
  0.6 4.1 %collective-permute-start = (bf16[1,192,256]{2,1,0:T(8,128)(2,1)}, bf16[1,192,256]{2,1,0:T(8,128)(2,1)S(1)}, u32[]{:S(2)}, u32[]{:S(2)}) collective-permute-start(bf16[1,192,256]{2,1,0:T(8,128)(2,1)} %bitcast.3), channel_id=1, source_target_pairs={{0,4},{1,5},{2,6},{3,7},{4,0},{5,1},{6,2},{7,3},{8,12},{9,13},{10,... | collective-permute-start | bytes 294920 | tf_op jit(solution)/shard_map/gather_far/ppermute | solution.py:430
  4.7 1.5 %collective-permute-start.2 = (bf16[48,256]{1,0:T(8,128)(2,1)}, bf16[48,256]{1,0:T(8,128)(2,1)S(1)}, u32[]{:S(2)}, u32[]{:S(2)}) collective-permute-start(bf16[48,256]{1,0:T(8,128)(2,1)} %refs_9_.1), channel_id=1, source_target_pairs={{0,16},{8,24},{16,0},{24,8},{1,17},{9,25},{17,1},{25,9},{2,18},{10... | collective-permute-start | bytes 73736 | tf_op jit(solution)/shard_map/gather_prefix/ppermute | solution.py:430
  6.6 1.6 %collective-permute-start.4 = (bf16[1,192,256]{2,1,0:T(8,128)(2,1)}, bf16[1,192,256]{2,1,0:T(8,128)(2,1)S(1)}, u32[]{:S(2)}, u32[]{:S(2)}) collective-permute-start(bf16[1,192,256]{2,1,0:T(8,128)(2,1)} %bitcast.4), channel_id=1, source_target_pairs={{0,2},{1,3},{2,0},{3,1},{4,6},{5,7},{6,4},{7,5},{8,10},{9,11},{10,... | collective-permute-start | bytes 294920 | tf_op jit(solution)/shard_map/gather_near/ppermute | solution.py:430
  8.2 1.5 %collective-permute-start.10 = (bf16[1,192,256]{2,1,0:T(8,128)(2,1)}, bf16[1,192,256]{2,1,0:T(8,128)(2,1)S(1)}, u32[]{:S(2)}, u32[]{:S(2)}) collective-permute-start(bf16[1,192,256]{2,1,0:T(8,128)(2,1)} %bitcast.5), channel_id=1, source_target_pairs={{0,1},{1,0},{2,3},{3,2},{4,5},{5,4},{6,7},{7,6},{8,9},{9,8},{10,11... | collective-permute-start | bytes 294920 | tf_op jit(solution)/shard_map/gather_own_x/ppermute | solution.py:430
  9.9 1.4 %collective-permute-start.9 = (bf16[1,192,256]{2,1,0:T(8,128)(2,1)S(1)}, bf16[1,192,256]{2,1,0:T(8,128)(2,1)S(1)}, u32[]{:S(2)}, u32[]{:S(2)}) collective-permute-start(bf16[1,192,256]{2,1,0:T(8,128)(2,1)S(1)} %collective-permute-done), channel_id=1, source_target_pairs={{0,2},{1,3},{2,0},{3,1},{4,6},{5,7},{6,4},{7,5},{8,10},{9,11},{10,... | collective-permute-start | bytes 294920 | tf_op jit(solution)/shard_map/gather_both/ppermute | solution.py:430
  12.0 1.6 %collective-permute-start.5 = (bf16[2,192,256]{2,1,0:T(8,128)(2,1)S(1)}, bf16[2,192,256]{2,1,0:T(8,128)(2,1)S(1)}, u32[]{:S(2)}, u32[]{:S(2)}) collective-permute-start(bf16[2,192,256]{2,1,0:T(8,128)(2,1)S(1)} %constant_dynamic-update-slice_fusion.refs_4_), channel_id=1, source_target_pairs={{0,1},{1,0},{2,3},{3,2},{4,5},{5,4},{6,7},{7,6},{8,9},{9,8},{10,11... | collective-permute-start | bytes 589832 | tf_op jit(solution)/shard_map/gather_pair_x/ppermute | solution.py:430
  13.6 2.7 %shard_map.139 = (s32[4]{0:T(128)S(4)}, s32[2]{0:T(128)S(4)}, s32[2]{0:T(128)S(4)}, bf16[192,256]{1,0:T(8,128)(2,1)S(1)}, bf16[192,128]{1,0:T(8,128)(2,1)S(1)}, ...) custom-call(s32[4]{0:T(128)} %refs_0_.1, ...), custom_call_target="tpu_custom_call" | custom-call | flops 2990000128 | tf_op jit(solution)/shard_map/pallas_call | solution.py:173
  16.9 1.0 %shard_map.140 = (bf16[2,1,192,80]{3,2,1,0:T(8,128)(2,1)S(1)}, bf16[2,1,192,96]{3,2,1,0:T(8,128)(2,1)S(1)}, f32[192,256]{1,0:T(8,128)S(1)}, bf16[192,256]{1,0:T(...) custom-call(s32[4]{0:T(128)S(4)} %get-tuple-element.44.refs_0_, ...), custom_call_target="tpu_custom_call" | custom-call | flops 1955000064 | tf_op jit(solution)/shard_map/pallas_call | solution.py:286
  17.9 1.5 %collective-permute-start.7 = (bf16[2,192,256]{2,1,0:T(8,128)(2,1)S(1)}, bf16[2,192,256]{2,1,0:T(8,128)(2,1)S(1)}, u32[]{:S(2)}, u32[]{:S(2)}) collective-permute-start(bf16[2,192,256]{2,1,0:T(8,128)(2,1)S(1)} %get-tuple-element.55), channel_id=1, source_target_pairs={{0,2},{1,3},{2,0},{3,1},{4,6},{5,7},{6,4},{7,5},{8,10},{9,11},{10,... | collective-permute-start | bytes 589832 | tf_op jit(solution)/shard_map/out_a/ppermute | solution.py:430
  20.0 1.0 %collective-permute-done.11.refs_8_ = bf16[1,192,256]{2,1,0:T(8,128)(2,1)S(1)} collective-permute-done((bf16[1,192,256]{2,1,0:T(8,128)(2,1)S(1)}, bf16[1,192,256]{2,1,0:T(8,128)(2,1)S(1)}, u32[]{:S(2)}, u32[]{:S(2)}) %collective-permute-start.11) | collective-permute-done | bytes 98336 | tf_op jit(solution)/shard_map/gather_both_x/ppermute | solution.py:430
  21.0 2.3 %shard_map.141 = (f32[2,48,256]{2,1,0:T(8,128)S(1)}, f32[2,48,256]{2,1,0:T(8,128)S(1)}, bf16[2,192,256]{2,1,0:T(8,128)(2,1)S(1)}, bf16[1,192,256]{2,1,0:T(8,128)...) custom-call(s32[4]{0:T(128)S(4)} %get-tuple-element.44.refs_0_, ...), custom_call_target="tpu_custom_call" | custom-call | flops 4024999936 | tf_op jit(solution)/shard_map/pallas_call | solution.py:382
  23.3 1.3 %collective-permute-start.13 = (bf16[2,192,256]{2,1,0:T(8,128)(2,1)S(1)}, bf16[2,192,256]{2,1,0:T(8,128)(2,1)S(1)}, u32[]{:S(2)}, u32[]{:S(2)}) collective-permute-start(bf16[2,192,256]{2,1,0:T(8,128)(2,1)S(1)} %get-tuple-element.71), channel_id=1, source_target_pairs={{0,1},{1,0},{2,3},{3,2},{4,5},{5,4},{6,7},{7,6},{8,9},{9,8},{10,11... | collective-permute-start | bytes 589832 | tf_op jit(solution)/shard_map/in_75/ppermute | solution.py:430
  24.7 1.1 %collective-permute-done.7 = bf16[2,192,256]{2,1,0:T(8,128)(2,1)S(1)} collective-permute-done((bf16[2,192,256]{2,1,0:T(8,128)(2,1)S(1)}, bf16[2,192,256]{2,1,0:T(8,128)(2,1)S(1)}, u32[]{:S(2)}, u32[]{:S(2)}) %collective-permute-start.7) | collective-permute-done | bytes 196640 | tf_op jit(solution)/shard_map/out_a/ppermute | solution.py:430
  25.8 2.2 %collective-permute-start.8 = (bf16[2,192,256]{2,1,0:T(8,128)(2,1)S(1)}, bf16[2,192,256]{2,1,0:T(8,128)(2,1)S(1)}, u32[]{:S(2)}, u32[]{:S(2)}) collective-permute-start(bf16[2,192,256]{2,1,0:T(8,128)(2,1)S(1)} %add_convert_fusion), channel_id=1, source_target_pairs={{0,4},{1,5},{2,6},{3,7},{4,0},{5,1},{6,2},{7,3},{8,12},{9,13},{10,... | collective-permute-start | bytes 589832 | tf_op jit(solution)/shard_map/out_mid/ppermute | solution.py:430
  28.0 1.5 %collective-permute-start.12 = (bf16[1,192,256]{2,1,0:T(8,128)(2,1)S(1)}, bf16[1,192,256]{2,1,0:T(8,128)(2,1)S(1)}, u32[]{:S(2)}, u32[]{:S(2)}) collective-permute-start(bf16[1,192,256]{2,1,0:T(8,128)(2,1)S(1)} %get-tuple-element.69), channel_id=1, source_target_pairs={{0,1},{1,0},{2,3},{3,2},{4,5},{5,4},{6,7},{7,6},{8,9},{9,8},{10,11... | collective-permute-start | bytes 294920 | tf_op jit(solution)/shard_map/in_3/ppermute | solution.py:430
  30.1 1.3 %collective-permute-start.14 = (bf16[1,192,256]{2,1,0:T(8,128)(2,1)S(1)}, bf16[1,192,256]{2,1,0:T(8,128)(2,1)S(1)}, u32[]{:S(2)}, u32[]{:S(2)}) collective-permute-start(bf16[1,192,256]{2,1,0:T(8,128)(2,1)S(1)} %add_convert_fusion.3), channel_id=1, source_target_pairs={{0,2},{1,3},{2,0},{3,1},{4,6},{5,7},{6,4},{7,5},{8,10},{9,11},{10,... | collective-permute-start | bytes 294920 | tf_op jit(solution)/shard_map/in_6/ppermute | solution.py:430
  31.4 1.2 %collective-permute-done.12 = bf16[1,192,256]{2,1,0:T(8,128)(2,1)S(1)} collective-permute-done((bf16[1,192,256]{2,1,0:T(8,128)(2,1)S(1)}, bf16[1,192,256]{2,1,0:T(8,128)(2,1)S(1)}, u32[]{:S(2)}, u32[]{:S(2)}) %collective-permute-start.12) | collective-permute-done | bytes 98336 | tf_op jit(solution)/shard_map/in_3/ppermute | solution.py:430
  32.6 1.7 %collective-permute-start.17 = (bf16[1,192,256]{2,1,0:T(8,128)(2,1)S(1)}, bf16[1,192,256]{2,1,0:T(8,128)(2,1)S(1)}, u32[]{:S(2)}, u32[]{:S(2)}) collective-permute-start(bf16[1,192,256]{2,1,0:T(8,128)(2,1)S(1)} %add_convert_fusion.4), channel_id=1, source_target_pairs={{0,2},{1,3},{2,0},{3,1},{4,6},{5,7},{6,4},{7,5},{8,10},{9,11},{10,... | collective-permute-start | bytes 294920 | tf_op jit(solution)/shard_map/in_2/ppermute | solution.py:430
  34.4 2.5 %collective-permute-start.16 = (bf16[1,192,256]{2,1,0:T(8,128)(2,1)S(1)}, bf16[1,192,256]{2,1,0:T(8,128)(2,1)S(1)}, u32[]{:S(2)}, u32[]{:S(2)}) collective-permute-start(bf16[1,192,256]{2,1,0:T(8,128)(2,1)S(1)} %get-tuple-element.77), channel_id=1, source_target_pairs={{0,1},{1,0},{2,3},{3,2},{4,5},{5,4},{6,7},{7,6},{8,9},{9,8},{10,11... | collective-permute-start | bytes 294920 | tf_op jit(solution)/shard_map/in_1/ppermute | solution.py:430
  36.9 1.3 %collective-permute-start.19 = (f32[2,48,256]{2,1,0:T(8,128)S(1)}, f32[2,48,256]{2,1,0:T(8,128)S(1)}, u32[]{:S(2)}, u32[]{:S(2)}) collective-permute-start(f32[2,48,256]{2,1,0:T(8,128)S(1)} %get-tuple-element.80), channel_id=1, source_target_pairs={{0,16},{8,24},{16,0},{24,8},{1,17},{9,25},{17,1},{25,9},{2,18},{10... | collective-permute-start | bytes 294920 | tf_op jit(solution)/shard_map/grad_prefix_y/ppermute | solution.py:430
  38.4 1.4 %collective-permute-start.15 = (bf16[1,192,256]{2,1,0:T(8,128)(2,1)S(1)}, bf16[1,192,256]{2,1,0:T(8,128)(2,1)S(1)}, u32[]{:S(2)}, u32[]{:S(2)}) collective-permute-start(bf16[1,192,256]{2,1,0:T(8,128)(2,1)S(1)} %add_convert_fusion.1), channel_id=1, source_target_pairs={{0,1},{1,0},{2,3},{3,2},{4,5},{5,4},{6,7},{7,6},{8,9},{9,8},{10,11... | collective-permute-start | bytes 294920 | tf_op jit(solution)/shard_map/out_x/ppermute | solution.py:430
  39.7 1.8 %collective-permute-done.19.refs_9_ = f32[2,48,256]{2,1,0:T(8,128)S(1)} collective-permute-done((f32[2,48,256]{2,1,0:T(8,128)S(1)}, f32[2,48,256]{2,1,0:T(8,128)S(1)}, u32[]{:S(2)}, u32[]{:S(2)}) %collective-permute-start.19) | collective-permute-done | bytes 98336 | tf_op jit(solution)/shard_map/grad_prefix_y/ppermute | solution.py:430
  41.6 1.2 %collective-permute-done.20.refs_10_ = f32[1,48,256]{2,1,0:T(8,128)S(1)} collective-permute-done((f32[1,48,256]{2,1,0:T(8,128)S(1)}, f32[1,48,256]{2,1,0:T(8,128)S(1)}, u32[]{:S(2)}, u32[]{:S(2)}) %collective-permute-start.20) | collective-permute-done | bytes 49184 | tf_op jit(solution)/shard_map/grad_prefix_core/ppermute | solution.py:430
  43.0 1.3 %collective-permute-done.18.refs_7_ = bf16[1,192,256]{2,1,0:T(8,128)(2,1)S(1)} collective-permute-done((bf16[1,192,256]{2,1,0:T(8,128)(2,1)S(1)}, bf16[1,192,256]{2,1,0:T(8,128)(2,1)S(1)}, u32[]{:S(2)}, u32[]{:S(2)}) %collective-permute-start.18) | collective-permute-done | bytes 98336 | tf_op jit(solution)/shard_map/in_4/ppermute | solution.py:430
  (32 shorter events, 4.4 us)
Async XLA Ops:
  0.6 9.2 %collective-permute-start = (bf16[1,192,256]{2,1,0:T(8,128)(2,1)}, bf16[1,192,256]{2,1,0:T(8,128)(2,1)S(1)}, u32[]{:S(2)}, u32[]{:S(2)}) collective-permute-start(bf16[1,192,256]{2,1,0:T(8,128)(2,1)} %bitcast.3), channel_id=1, source_target_pairs={{0,4},{1,5},{2,6},{3,7},{4,0},{5,1},{6,2},{7,3},{8,12},{9,13},{10,... | collective-permute-start | bytes 294920 | tf_op jit(solution)/shard_map/gather_far/ppermute | solution.py:430
  4.7 3.4 %collective-permute-start.1 = (bf16[48,256]{1,0:T(8,128)(2,1)}, bf16[48,256]{1,0:T(8,128)(2,1)S(1)}, u32[]{:S(2)}, u32[]{:S(2)}) collective-permute-start(bf16[48,256]{1,0:T(8,128)(2,1)} %refs_9_.1), channel_id=1, source_target_pairs={{0,8},{8,0},{16,24},{24,16},{1,9},{9,1},{17,25},{25,17},{2,10},{10... | collective-permute-start | bytes 73736 | tf_op jit(solution)/shard_map/gather_prefix/ppermute | solution.py:430
  4.7 4.9 %collective-permute-start.2 = (bf16[48,256]{1,0:T(8,128)(2,1)}, bf16[48,256]{1,0:T(8,128)(2,1)S(1)}, u32[]{:S(2)}, u32[]{:S(2)}) collective-permute-start(bf16[48,256]{1,0:T(8,128)(2,1)} %refs_9_.1), channel_id=1, source_target_pairs={{0,16},{8,24},{16,0},{24,8},{1,17},{9,25},{17,1},{25,9},{2,18},{10... | collective-permute-start | bytes 73736 | tf_op jit(solution)/shard_map/gather_prefix/ppermute | solution.py:430
  6.3 3.5 %collective-permute-start.3 = (bf16[48,256]{1,0:T(8,128)(2,1)}, bf16[48,256]{1,0:T(8,128)(2,1)S(1)}, u32[]{:S(2)}, u32[]{:S(2)}) collective-permute-start(bf16[48,256]{1,0:T(8,128)(2,1)} %refs_9_.1), channel_id=1, source_target_pairs={{0,24},{8,16},{16,8},{24,0},{1,25},{9,17},{17,9},{25,1},{2,26},{10... | collective-permute-start | bytes 73736 | tf_op jit(solution)/shard_map/gather_prefix/ppermute | solution.py:430
  6.6 5.4 %collective-permute-start.4 = (bf16[1,192,256]{2,1,0:T(8,128)(2,1)}, bf16[1,192,256]{2,1,0:T(8,128)(2,1)S(1)}, u32[]{:S(2)}, u32[]{:S(2)}) collective-permute-start(bf16[1,192,256]{2,1,0:T(8,128)(2,1)} %bitcast.4), channel_id=1, source_target_pairs={{0,2},{1,3},{2,0},{3,1},{4,6},{5,7},{6,4},{7,5},{8,10},{9,11},{10,... | collective-permute-start | bytes 294920 | tf_op jit(solution)/shard_map/gather_near/ppermute | solution.py:430
  8.2 11.8 %collective-permute-start.10 = (bf16[1,192,256]{2,1,0:T(8,128)(2,1)}, bf16[1,192,256]{2,1,0:T(8,128)(2,1)S(1)}, u32[]{:S(2)}, u32[]{:S(2)}) collective-permute-start(bf16[1,192,256]{2,1,0:T(8,128)(2,1)} %bitcast.5), channel_id=1, source_target_pairs={{0,1},{1,0},{2,3},{3,2},{4,5},{5,4},{6,7},{7,6},{8,9},{9,8},{10,11... | collective-permute-start | bytes 294920 | tf_op jit(solution)/shard_map/gather_own_x/ppermute | solution.py:430
  9.9 6.4 %collective-permute-start.9 = (bf16[1,192,256]{2,1,0:T(8,128)(2,1)S(1)}, bf16[1,192,256]{2,1,0:T(8,128)(2,1)S(1)}, u32[]{:S(2)}, u32[]{:S(2)}) collective-permute-start(bf16[1,192,256]{2,1,0:T(8,128)(2,1)S(1)} %collective-permute-done), channel_id=1, source_target_pairs={{0,2},{1,3},{2,0},{3,1},{4,6},{5,7},{6,4},{7,5},{8,10},{9,11},{10,... | collective-permute-start | bytes 294920 | tf_op jit(solution)/shard_map/gather_both/ppermute | solution.py:430
  12.0 7.4 %collective-permute-start.5 = (bf16[2,192,256]{2,1,0:T(8,128)(2,1)S(1)}, bf16[2,192,256]{2,1,0:T(8,128)(2,1)S(1)}, u32[]{:S(2)}, u32[]{:S(2)}) collective-permute-start(bf16[2,192,256]{2,1,0:T(8,128)(2,1)S(1)} %constant_dynamic-update-slice_fusion.refs_4_), channel_id=1, source_target_pairs={{0,1},{1,0},{2,3},{3,2},{4,5},{5,4},{6,7},{7,6},{8,9},{9,8},{10,11... | collective-permute-start | bytes 589832 | tf_op jit(solution)/shard_map/gather_pair_x/ppermute | solution.py:430
  13.6 3.3 %copy-start = (bf16[256,2048]{1,0:T(8,128)(2,1)S(1)}, bf16[256,2048]{1,0:T(8,128)(2,1)}, u32[]{:S(2)}) copy-start(bf16[256,2048]{1,0:T(8,128)(2,1)} %refs_17_.1) | copy-start | bytes 3145732
  16.3 4.7 %collective-permute-start.11 = (bf16[1,192,256]{2,1,0:T(8,128)(2,1)S(1)}, bf16[1,192,256]{2,1,0:T(8,128)(2,1)S(1)}, u32[]{:S(2)}, u32[]{:S(2)}) collective-permute-start(bf16[1,192,256]{2,1,0:T(8,128)(2,1)S(1)} %collective-permute-done.9.refs_5_), channel_id=1, source_target_pairs={{0,1},{1,0},{2,3},{3,2},{4,5},{5,4},{6,7},{7,6},{8,9},{9,8},{10,11... | collective-permute-start | bytes 294920 | tf_op jit(solution)/shard_map/gather_both_x/ppermute | solution.py:430
  17.9 7.9 %collective-permute-start.7 = (bf16[2,192,256]{2,1,0:T(8,128)(2,1)S(1)}, bf16[2,192,256]{2,1,0:T(8,128)(2,1)S(1)}, u32[]{:S(2)}, u32[]{:S(2)}) collective-permute-start(bf16[2,192,256]{2,1,0:T(8,128)(2,1)S(1)} %get-tuple-element.55), channel_id=1, source_target_pairs={{0,2},{1,3},{2,0},{3,1},{4,6},{5,7},{6,4},{7,5},{8,10},{9,11},{10,... | collective-permute-start | bytes 589832 | tf_op jit(solution)/shard_map/out_a/ppermute | solution.py:430
  19.3 17.5 %collective-permute-start.6 = (bf16[2,192,256]{2,1,0:T(8,128)(2,1)S(1)}, bf16[2,192,256]{2,1,0:T(8,128)(2,1)S(1)}, u32[]{:S(2)}, u32[]{:S(2)}) collective-permute-start(bf16[2,192,256]{2,1,0:T(8,128)(2,1)S(1)} %get-tuple-element.53), channel_id=1, source_target_pairs={{0,2},{1,3},{2,0},{3,1},{4,6},{5,7},{6,4},{7,5},{8,10},{9,11},{10,... | collective-permute-start | bytes 589832 | tf_op jit(solution)/shard_map/out_b/ppermute | solution.py:430
  23.3 6.8 %collective-permute-start.13 = (bf16[2,192,256]{2,1,0:T(8,128)(2,1)S(1)}, bf16[2,192,256]{2,1,0:T(8,128)(2,1)S(1)}, u32[]{:S(2)}, u32[]{:S(2)}) collective-permute-start(bf16[2,192,256]{2,1,0:T(8,128)(2,1)S(1)} %get-tuple-element.71), channel_id=1, source_target_pairs={{0,1},{1,0},{2,3},{3,2},{4,5},{5,4},{6,7},{7,6},{8,9},{9,8},{10,11... | collective-permute-start | bytes 589832 | tf_op jit(solution)/shard_map/in_75/ppermute | solution.py:430
  25.8 12.4 %collective-permute-start.8 = (bf16[2,192,256]{2,1,0:T(8,128)(2,1)S(1)}, bf16[2,192,256]{2,1,0:T(8,128)(2,1)S(1)}, u32[]{:S(2)}, u32[]{:S(2)}) collective-permute-start(bf16[2,192,256]{2,1,0:T(8,128)(2,1)S(1)} %add_convert_fusion), channel_id=1, source_target_pairs={{0,4},{1,5},{2,6},{3,7},{4,0},{5,1},{6,2},{7,3},{8,12},{9,13},{10,... | collective-permute-start | bytes 589832 | tf_op jit(solution)/shard_map/out_mid/ppermute | solution.py:430
  28.0 4.6 %collective-permute-start.12 = (bf16[1,192,256]{2,1,0:T(8,128)(2,1)S(1)}, bf16[1,192,256]{2,1,0:T(8,128)(2,1)S(1)}, u32[]{:S(2)}, u32[]{:S(2)}) collective-permute-start(bf16[1,192,256]{2,1,0:T(8,128)(2,1)S(1)} %get-tuple-element.69), channel_id=1, source_target_pairs={{0,1},{1,0},{2,3},{3,2},{4,5},{5,4},{6,7},{7,6},{8,9},{9,8},{10,11... | collective-permute-start | bytes 294920 | tf_op jit(solution)/shard_map/in_3/ppermute | solution.py:430
  30.1 8.0 %collective-permute-start.14 = (bf16[1,192,256]{2,1,0:T(8,128)(2,1)S(1)}, bf16[1,192,256]{2,1,0:T(8,128)(2,1)S(1)}, u32[]{:S(2)}, u32[]{:S(2)}) collective-permute-start(bf16[1,192,256]{2,1,0:T(8,128)(2,1)S(1)} %add_convert_fusion.3), channel_id=1, source_target_pairs={{0,2},{1,3},{2,0},{3,1},{4,6},{5,7},{6,4},{7,5},{8,10},{9,11},{10,... | collective-permute-start | bytes 294920 | tf_op jit(solution)/shard_map/in_6/ppermute | solution.py:430
  32.6 8.9 %collective-permute-start.17 = (bf16[1,192,256]{2,1,0:T(8,128)(2,1)S(1)}, bf16[1,192,256]{2,1,0:T(8,128)(2,1)S(1)}, u32[]{:S(2)}, u32[]{:S(2)}) collective-permute-start(bf16[1,192,256]{2,1,0:T(8,128)(2,1)S(1)} %add_convert_fusion.4), channel_id=1, source_target_pairs={{0,2},{1,3},{2,0},{3,1},{4,6},{5,7},{6,4},{7,5},{8,10},{9,11},{10,... | collective-permute-start | bytes 294920 | tf_op jit(solution)/shard_map/in_2/ppermute | solution.py:430
  34.4 7.2 %collective-permute-start.16 = (bf16[1,192,256]{2,1,0:T(8,128)(2,1)S(1)}, bf16[1,192,256]{2,1,0:T(8,128)(2,1)S(1)}, u32[]{:S(2)}, u32[]{:S(2)}) collective-permute-start(bf16[1,192,256]{2,1,0:T(8,128)(2,1)S(1)} %get-tuple-element.77), channel_id=1, source_target_pairs={{0,1},{1,0},{2,3},{3,2},{4,5},{5,4},{6,7},{7,6},{8,9},{9,8},{10,11... | collective-permute-start | bytes 294920 | tf_op jit(solution)/shard_map/in_1/ppermute | solution.py:430
  36.9 4.6 %collective-permute-start.19 = (f32[2,48,256]{2,1,0:T(8,128)S(1)}, f32[2,48,256]{2,1,0:T(8,128)S(1)}, u32[]{:S(2)}, u32[]{:S(2)}) collective-permute-start(f32[2,48,256]{2,1,0:T(8,128)S(1)} %get-tuple-element.80), channel_id=1, source_target_pairs={{0,16},{8,24},{16,0},{24,8},{1,17},{9,25},{17,1},{25,9},{2,18},{10... | collective-permute-start | bytes 294920 | tf_op jit(solution)/shard_map/grad_prefix_y/ppermute | solution.py:430
  38.2 6.1 %collective-permute-start.18 = (bf16[1,192,256]{2,1,0:T(8,128)(2,1)S(1)}, bf16[1,192,256]{2,1,0:T(8,128)(2,1)S(1)}, u32[]{:S(2)}, u32[]{:S(2)}) collective-permute-start(bf16[1,192,256]{2,1,0:T(8,128)(2,1)S(1)} %add_convert_fusion.2), channel_id=1, source_target_pairs={{0,4},{1,5},{2,6},{3,7},{4,0},{5,1},{6,2},{7,3},{8,12},{9,13},{10,... | collective-permute-start | bytes 294920 | tf_op jit(solution)/shard_map/in_4/ppermute | solution.py:430
  38.4 4.7 %collective-permute-start.15 = (bf16[1,192,256]{2,1,0:T(8,128)(2,1)S(1)}, bf16[1,192,256]{2,1,0:T(8,128)(2,1)S(1)}, u32[]{:S(2)}, u32[]{:S(2)}) collective-permute-start(bf16[1,192,256]{2,1,0:T(8,128)(2,1)S(1)} %add_convert_fusion.1), channel_id=1, source_target_pairs={{0,1},{1,0},{2,3},{3,2},{4,5},{5,4},{6,7},{7,6},{8,9},{9,8},{10,11... | collective-permute-start | bytes 294920 | tf_op jit(solution)/shard_map/out_x/ppermute | solution.py:430
  41.5 1.3 %collective-permute-start.20 = (f32[1,48,256]{2,1,0:T(8,128)S(1)}, f32[1,48,256]{2,1,0:T(8,128)S(1)}, u32[]{:S(2)}, u32[]{:S(2)}) collective-permute-start(f32[1,48,256]{2,1,0:T(8,128)S(1)} %slice_add_fusion), channel_id=1, source_target_pairs={{0,8},{8,0},{16,24},{24,16},{1,9},{9,1},{17,25},{25,17},{2,10},{10... | collective-permute-start | bytes 147464 | tf_op jit(solution)/shard_map/grad_prefix_core/ppermute | solution.py:430

commit v3 on v0

--- a/solution.py
+++ b/solution.py
@@ -13,7 +13,8 @@
 HELD = ((0,), (4, 2), (6,), (1,), (5, 3), (7,))
 OUT = ((6, 7), (2, 3), (4, 5), (0, 1))
 TERMS = ((1, 3), (0, 2))
-IN = ((7, 5), (3,), (1,), (6,), (4,), (2,), (0,))
+IN_FIRST = ((7, 5),)
+IN_REST = ((3,), (1,), (6,), (4,), (2,), (0,))
 F32 = jnp.float32
 BF16 = jnp.bfloat16
 HBM = pl.BlockSpec(memory_space=pltpu.HBM)
@@ -304,7 +305,7 @@
     p_pre, p_own, heads_out, prefix_v = take(4)
     terms = take(len(rest) - len(names) - 2)
     parts = take(len(names))
-    grad_prefix, grads = take(2)
+    grads, grad_prefix = take(2)
 
     width = cotangent[0].shape[2]
     me = lax.axis_index("mp")
@@ -379,19 +380,38 @@
     k_width = key.shape[1]
     count, kv_width = prefix.shape
     results = [(x, F32) for x in terms] + block_shapes(names, rows, cotangent[0].shape[2])
+    results.append(((rows, q_width + 2 * k_width), BF16))
     found = pl.pallas_call(
         functools.partial(backward_kernel, slots, names),
         in_specs=[SMEM] * 3 + [VMEM] * (len(cotangent) + len(kept)),
         out_specs=[VMEM] * len(results),
         out_shape=in_vmem(results),
-        scratch_shapes=[
-            pltpu.VMEM((count, kv_width), F32),
-            pltpu.VMEM((rows, q_width + 2 * k_width), BF16),
-        ],
+        scratch_shapes=[pltpu.VMEM((count, kv_width), F32)],
         compiler_params=pltpu.CompilerParams(vmem_limit_bytes=vmem_room(count)),
-        cost_estimate=lasting(3.5),
+        cost_estimate=lasting(2.5),
     )(*held_in(pltpu.SMEM, scalars), *held_in(pltpu.VMEM, [*cotangent, *kept]))
-    return found[: len(terms)], found[len(terms) :]
+    return found[: len(terms)], found[len(terms) : -1], found[-1]
+
+
+def rest_kernel(names, *refs):
+    grads, w_all, *parts = refs
+
+    def make(cols):
+        return dot_nt(grads[...], w_all[cols, :]).astype(BF16)
+
+    make_blocks(make, names, parts)
+
+
+def rest(names, width, grads, w_all):
+    results = block_shapes(names, grads.shape[0], width)
+    return pl.pallas_call(
+        functools.partial(rest_kernel, names),
+        in_specs=[VMEM] * 2,
+        out_specs=[VMEM] * len(results),
+        out_shape=in_vmem(results),
+        compiler_params=pltpu.CompilerParams(vmem_limit_bytes=vmem_room(0)),
+        cost_estimate=lasting(0.7),
+    )(*held_in(pltpu.VMEM, [grads, w_all]))
 
 
 def last_kernel(counts, *refs):
@@ -481,14 +501,15 @@
     back = [own, pair, both, own_x, pair_x, both_x]
     shape = prefix_kv.shape
     terms = [(1, *shape)] if chips != 4 else [(len(steps), *shape) for steps in TERMS]
-    terms, grads = backward(IN, scalars, back, [*projected, *weights, w_out, *probed], terms)
+    kept = [*projected, *weights, w_out, *probed]
+    terms, (in_75,), grads = backward(IN_FIRST, scalars, back, kept, terms)
+    in_3, in_1, in_6, in_4, in_2, in_0 = rest(IN_REST, cotangent.shape[1], grads, weights[0])
 
     out_a, out_b, kept_a, kept_b = parts
     got_a = trade("out_a", out_a, "mp", 2)
     got_b = trade("out_b", after(out_b, pair_x), "mp", 2)
     out_a = total(kept_a, got_a)
     got_out = trade("out_mid", out_a, "mp", 4)
-    in_75, in_3, in_1, in_6, in_4, in_2, in_0 = grads
     got_75 = trade("in_75", in_75, "mp", 1)
     got_3 = trade("in_3", in_3, "mp", 1)
     in_6 = total(after(in_6, out_a), got_75[:1])

time: 44.8 us -> 45 us (level)
  waiting for transfers between devices: 8.73 us -> 7.83 us
  starting transfers between devices: 28.3 us -> 29.2 us
    ppermute x21, waiting for transfers between devices: 8.73 us -> 7.83 us  [trade(): lax.ppermute(block, axis, [(i, i ^ step) for i in range(lax.axis_size(axi...]
    ppermute x21, starting transfers between devices: 28.3 us -> 29.2 us  [trade(): lax.ppermute(block, axis, [(i, i ^ step) for i in range(lax.axis_size(axi...]
    pallas_call x0 -> x1, Pallas kernels: none -> 0.67 us  [rest(): pl.pallas_call(functools.partial(rest_kernel, names), in_specs=[VMEM] * 2...]
    pallas_call x1, Pallas kernels: 2.32 us -> 1.82 us  [backward(): pl.pallas_call(functools.partial(backward_kernel, slots, names), in_specs...]
  transfers between devices with their start and end apart: 21 -> 21, of which waited for: 9 -> 7; matrix products, arithmetic and copies ran while one was open for 0% -> 0% of each run, Pallas kernels for 13% -> 14%
where the time goes in v3:
time: 45 us; the launch traced here: 44.8 us
  starting transfers between devices  29.2 us (65%)
  waiting for transfers between devices  7.83 us (17%)
  Pallas kernels  6.86 us (15%)
  between operations  0.72 us (2%)
    ppermute x21, starting transfers between devices, trade(): lax.ppermute(block, axis, [(i, i ^ step) for i in range(lax.axis_size(axi...  29.2 us
    ppermute x21, waiting for transfers between devices, trade(): lax.ppermute(block, axis, [(i, i ^ step) for i in range(lax.axis_size(axi...  7.83 us
    pallas_call x1, Pallas kernels, project(): pl.pallas_call(project_kernel, in_specs=[HBM] * len(operands), out_specs=...  2.63 us
    pallas_call x1, Pallas kernels, backward(): pl.pallas_call(functools.partial(backward_kernel, slots, names), in_specs...  1.82 us
    pallas_call x1, Pallas kernels, forward(): pl.pallas_call(functools.partial(forward_kernel, slots, names), in_specs=...  0.97 us
  transfers between devices with their start and end apart: 21, of which 7 were waited for; matrix products, arithmetic and copies ran while one was open for 0% of the time, Pallas kernels for 14%

profile of v3, /device:TPU:0, one launch (start us, length us, event | category | flops | bytes accessed | tf_op | source)
XLA Modules:
  0.0 44.8 jit_solution(18422101875132113984)
XLA Ops:
  0.6 4.1 %collective-permute-start = (bf16[1,192,256]{2,1,0:T(8,128)(2,1)}, bf16[1,192,256]{2,1,0:T(8,128)(2,1)S(1)}, u32[]{:S(2)}, u32[]{:S(2)}) collective-permute-start(bf16[1,192,256]{2,1,0:T(8,128)(2,1)} %bitcast.3), channel_id=1, source_target_pairs={{0,4},{1,5},{2,6},{3,7},{4,0},{5,1},{6,2},{7,3},{8,12},{9,13},{10,... | collective-permute-start | bytes 294920 | tf_op jit(solution)/shard_map/gather_far/ppermute | solution.py:450
  4.7 1.5 %collective-permute-start.2 = (bf16[48,256]{1,0:T(8,128)(2,1)}, bf16[48,256]{1,0:T(8,128)(2,1)S(1)}, u32[]{:S(2)}, u32[]{:S(2)}) collective-permute-start(bf16[48,256]{1,0:T(8,128)(2,1)} %refs_9_.1), channel_id=1, source_target_pairs={{0,16},{8,24},{16,0},{24,8},{1,17},{9,25},{17,1},{25,9},{2,18},{10... | collective-permute-start | bytes 73736 | tf_op jit(solution)/shard_map/gather_prefix/ppermute | solution.py:450
  6.6 1.6 %collective-permute-start.4 = (bf16[1,192,256]{2,1,0:T(8,128)(2,1)}, bf16[1,192,256]{2,1,0:T(8,128)(2,1)S(1)}, u32[]{:S(2)}, u32[]{:S(2)}) collective-permute-start(bf16[1,192,256]{2,1,0:T(8,128)(2,1)} %bitcast.4), channel_id=1, source_target_pairs={{0,2},{1,3},{2,0},{3,1},{4,6},{5,7},{6,4},{7,5},{8,10},{9,11},{10,... | collective-permute-start | bytes 294920 | tf_op jit(solution)/shard_map/gather_near/ppermute | solution.py:450
  8.2 1.5 %collective-permute-start.10 = (bf16[1,192,256]{2,1,0:T(8,128)(2,1)}, bf16[1,192,256]{2,1,0:T(8,128)(2,1)S(1)}, u32[]{:S(2)}, u32[]{:S(2)}) collective-permute-start(bf16[1,192,256]{2,1,0:T(8,128)(2,1)} %bitcast.5), channel_id=1, source_target_pairs={{0,1},{1,0},{2,3},{3,2},{4,5},{5,4},{6,7},{7,6},{8,9},{9,8},{10,11... | collective-permute-start | bytes 294920 | tf_op jit(solution)/shard_map/gather_own_x/ppermute | solution.py:450
  9.9 1.4 %collective-permute-start.9 = (bf16[1,192,256]{2,1,0:T(8,128)(2,1)S(1)}, bf16[1,192,256]{2,1,0:T(8,128)(2,1)S(1)}, u32[]{:S(2)}, u32[]{:S(2)}) collective-permute-start(bf16[1,192,256]{2,1,0:T(8,128)(2,1)S(1)} %collective-permute-done), channel_id=1, source_target_pairs={{0,2},{1,3},{2,0},{3,1},{4,6},{5,7},{6,4},{7,5},{8,10},{9,11},{10,... | collective-permute-start | bytes 294920 | tf_op jit(solution)/shard_map/gather_both/ppermute | solution.py:450
  12.0 1.6 %collective-permute-start.5 = (bf16[2,192,256]{2,1,0:T(8,128)(2,1)S(1)}, bf16[2,192,256]{2,1,0:T(8,128)(2,1)S(1)}, u32[]{:S(2)}, u32[]{:S(2)}) collective-permute-start(bf16[2,192,256]{2,1,0:T(8,128)(2,1)S(1)} %constant_dynamic-update-slice_fusion.refs_4_), channel_id=1, source_target_pairs={{0,1},{1,0},{2,3},{3,2},{4,5},{5,4},{6,7},{7,6},{8,9},{9,8},{10,11... | collective-permute-start | bytes 589832 | tf_op jit(solution)/shard_map/gather_pair_x/ppermute | solution.py:450
  13.6 2.6 %shard_map.139 = (s32[4]{0:T(128)S(4)}, s32[2]{0:T(128)S(4)}, s32[2]{0:T(128)S(4)}, bf16[192,256]{1,0:T(8,128)(2,1)S(1)}, bf16[192,128]{1,0:T(8,128)(2,1)S(1)}, ...) custom-call(s32[4]{0:T(128)} %refs_0_.1, ...), custom_call_target="tpu_custom_call" | custom-call | flops 2990000128 | tf_op jit(solution)/shard_map/pallas_call | solution.py:174
  16.8 1.0 %shard_map.140 = (bf16[2,1,192,80]{3,2,1,0:T(8,128)(2,1)S(1)}, bf16[2,1,192,96]{3,2,1,0:T(8,128)(2,1)S(1)}, f32[192,256]{1,0:T(8,128)S(1)}, bf16[192,256]{1,0:T(...) custom-call(s32[4]{0:T(128)S(4)} %get-tuple-element.45.refs_0_, ...), custom_call_target="tpu_custom_call" | custom-call | flops 1955000064 | tf_op jit(solution)/shard_map/pallas_call | solution.py:287
  17.7 1.5 %collective-permute-start.7 = (bf16[2,192,256]{2,1,0:T(8,128)(2,1)S(1)}, bf16[2,192,256]{2,1,0:T(8,128)(2,1)S(1)}, u32[]{:S(2)}, u32[]{:S(2)}) collective-permute-start(bf16[2,192,256]{2,1,0:T(8,128)(2,1)S(1)} %get-tuple-element.56), channel_id=1, source_target_pairs={{0,2},{1,3},{2,0},{3,1},{4,6},{5,7},{6,4},{7,5},{8,10},{9,11},{10,... | collective-permute-start | bytes 589832 | tf_op jit(solution)/shard_map/out_a/ppermute | solution.py:450
  19.9 1.0 %collective-permute-done.11.refs_8_ = bf16[1,192,256]{2,1,0:T(8,128)(2,1)S(1)} collective-permute-done((bf16[1,192,256]{2,1,0:T(8,128)(2,1)S(1)}, bf16[1,192,256]{2,1,0:T(8,128)(2,1)S(1)}, u32[]{:S(2)}, u32[]{:S(2)}) %collective-permute-start.11) | collective-permute-done | bytes 98336 | tf_op jit(solution)/shard_map/gather_both_x/ppermute | solution.py:450
  20.9 1.8 %shard_map.141 = (f32[2,48,256]{2,1,0:T(8,128)S(1)}, f32[2,48,256]{2,1,0:T(8,128)S(1)}, bf16[2,192,256]{2,1,0:T(8,128)(2,1)S(1)}, bf16[192,512]{1,0:T(8,128)(2,1)S(1)}) custom-call(s32[4]{0:T(128)S(4)} %get-tuple-element.45.refs_0_, s32[2]{0:T(128)S(4)} %get-tuple-element.46.refs_1_, s32[2]{0:T(128)S(4)} %get-tuple-element.47.refs_2_, ...), custom_call_target="tpu_custom_call" | custom-call | flops 2875000064 | tf_op jit(solution)/shard_map/pallas_call | solution.py:384
  22.7 1.4 %collective-permute-start.13 = (bf16[2,192,256]{2,1,0:T(8,128)(2,1)S(1)}, bf16[2,192,256]{2,1,0:T(8,128)(2,1)S(1)}, u32[]{:S(2)}, u32[]{:S(2)}) collective-permute-start(bf16[2,192,256]{2,1,0:T(8,128)(2,1)S(1)} %get-tuple-element.73), channel_id=1, source_target_pairs={{0,1},{1,0},{2,3},{3,2},{4,5},{5,4},{6,7},{7,6},{8,9},{9,8},{10,11... | collective-permute-start | bytes 589832 | tf_op jit(solution)/shard_map/in_75/ppermute | solution.py:450
  24.2 1.5 %collective-permute-done.7 = bf16[2,192,256]{2,1,0:T(8,128)(2,1)S(1)} collective-permute-done((bf16[2,192,256]{2,1,0:T(8,128)(2,1)S(1)}, bf16[2,192,256]{2,1,0:T(8,128)(2,1)S(1)}, u32[]{:S(2)}, u32[]{:S(2)}) %collective-permute-start.7) | collective-permute-done | bytes 196640 | tf_op jit(solution)/shard_map/out_a/ppermute | solution.py:450
  25.7 2.2 %collective-permute-start.8 = (bf16[2,192,256]{2,1,0:T(8,128)(2,1)S(1)}, bf16[2,192,256]{2,1,0:T(8,128)(2,1)S(1)}, u32[]{:S(2)}, u32[]{:S(2)}) collective-permute-start(bf16[2,192,256]{2,1,0:T(8,128)(2,1)S(1)} %add_convert_fusion), channel_id=1, source_target_pairs={{0,4},{1,5},{2,6},{3,7},{4,0},{5,1},{6,2},{7,3},{8,12},{9,13},{10,... | collective-permute-start | bytes 589832 | tf_op jit(solution)/shard_map/out_mid/ppermute | solution.py:450
  28.6 1.5 %collective-permute-start.12 = (bf16[1,192,256]{2,1,0:T(8,128)(2,1)S(1)}, bf16[1,192,256]{2,1,0:T(8,128)(2,1)S(1)}, u32[]{:S(2)}, u32[]{:S(2)}) collective-permute-start(bf16[1,192,256]{2,1,0:T(8,128)(2,1)S(1)} %get-tuple-element.71), channel_id=1, source_target_pairs={{0,1},{1,0},{2,3},{3,2},{4,5},{5,4},{6,7},{7,6},{8,9},{9,8},{10,11... | collective-permute-start | bytes 294920 | tf_op jit(solution)/shard_map/in_3/ppermute | solution.py:450
  30.2 1.7 %collective-permute-start.14 = (bf16[1,192,256]{2,1,0:T(8,128)(2,1)S(1)}, bf16[1,192,256]{2,1,0:T(8,128)(2,1)S(1)}, u32[]{:S(2)}, u32[]{:S(2)}) collective-permute-start(bf16[1,192,256]{2,1,0:T(8,128)(2,1)S(1)} %add_convert_fusion.3), channel_id=1, source_target_pairs={{0,2},{1,3},{2,0},{3,1},{4,6},{5,7},{6,4},{7,5},{8,10},{9,11},{10,... | collective-permute-start | bytes 294920 | tf_op jit(solution)/shard_map/in_6/ppermute | solution.py:450
  31.9 1.4 %collective-permute-done.12 = bf16[1,192,256]{2,1,0:T(8,128)(2,1)S(1)} collective-permute-done((bf16[1,192,256]{2,1,0:T(8,128)(2,1)S(1)}, bf16[1,192,256]{2,1,0:T(8,128)(2,1)S(1)}, u32[]{:S(2)}, u32[]{:S(2)}) %collective-permute-start.12) | collective-permute-done | bytes 98336 | tf_op jit(solution)/shard_map/in_3/ppermute | solution.py:450
  33.3 1.7 %collective-permute-start.17 = (bf16[1,192,256]{2,1,0:T(8,128)(2,1)S(1)}, bf16[1,192,256]{2,1,0:T(8,128)(2,1)S(1)}, u32[]{:S(2)}, u32[]{:S(2)}) collective-permute-start(bf16[1,192,256]{2,1,0:T(8,128)(2,1)S(1)} %add_convert_fusion.4), channel_id=1, source_target_pairs={{0,2},{1,3},{2,0},{3,1},{4,6},{5,7},{6,4},{7,5},{8,10},{9,11},{10,... | collective-permute-start | bytes 294920 | tf_op jit(solution)/shard_map/in_2/ppermute | solution.py:450
  35.7 2.0 %collective-permute-start.18 = (bf16[1,192,256]{2,1,0:T(8,128)(2,1)S(1)}, bf16[1,192,256]{2,1,0:T(8,128)(2,1)S(1)}, u32[]{:S(2)}, u32[]{:S(2)}) collective-permute-start(bf16[1,192,256]{2,1,0:T(8,128)(2,1)S(1)} %add_convert_fusion.2), channel_id=1, source_target_pairs={{0,4},{1,5},{2,6},{3,7},{4,0},{5,1},{6,2},{7,3},{8,12},{9,13},{10,... | collective-permute-start | bytes 294920 | tf_op jit(solution)/shard_map/in_4/ppermute | solution.py:450
  37.8 1.4 %collective-permute-start.15 = (bf16[1,192,256]{2,1,0:T(8,128)(2,1)S(1)}, bf16[1,192,256]{2,1,0:T(8,128)(2,1)S(1)}, u32[]{:S(2)}, u32[]{:S(2)}) collective-permute-start(bf16[1,192,256]{2,1,0:T(8,128)(2,1)S(1)} %add_convert_fusion.1), channel_id=1, source_target_pairs={{0,1},{1,0},{2,3},{3,2},{4,5},{5,4},{6,7},{7,6},{8,9},{9,8},{10,11... | collective-permute-start | bytes 294920 | tf_op jit(solution)/shard_map/out_x/ppermute | solution.py:450
  39.1 0.7 %collective-permute-start.16 = (bf16[1,192,256]{2,1,0:T(8,128)(2,1)S(1)}, bf16[1,192,256]{2,1,0:T(8,128)(2,1)S(1)}, u32[]{:S(2)}, u32[]{:S(2)}) collective-permute-start(bf16[1,192,256]{2,1,0:T(8,128)(2,1)S(1)} %get-tuple-element.79), channel_id=1, source_target_pairs={{0,1},{1,0},{2,3},{3,2},{4,5},{5,4},{6,7},{7,6},{8,9},{9,8},{10,11... | collective-permute-start | bytes 294920 | tf_op jit(solution)/shard_map/in_1/ppermute | solution.py:450
  39.9 1.7 %collective-permute-start.20 = (f32[1,48,256]{2,1,0:T(8,128)S(1)}, f32[1,48,256]{2,1,0:T(8,128)S(1)}, u32[]{:S(2)}, u32[]{:S(2)}) collective-permute-start(f32[1,48,256]{2,1,0:T(8,128)S(1)} %slice_add_fusion), channel_id=1, source_target_pairs={{0,16},{8,24},{16,0},{24,8},{1,17},{9,25},{17,1},{25,9},{2,18},{10... | collective-permute-start | bytes 147464 | tf_op jit(solution)/shard_map/grad_prefix_y/ppermute | solution.py:450
  41.6 2.5 %collective-permute-done.20.refs_10_ = f32[1,48,256]{2,1,0:T(8,128)S(1)} collective-permute-done((f32[1,48,256]{2,1,0:T(8,128)S(1)}, f32[1,48,256]{2,1,0:T(8,128)S(1)}, u32[]{:S(2)}, u32[]{:S(2)}) %collective-permute-start.20) | collective-permute-done | bytes 49184 | tf_op jit(solution)/shard_map/grad_prefix_y/ppermute | solution.py:450
  44.1 0.8 %shard_map.143 = (bf16[192,256]{1,0:T(8,128)(2,1)}, bf16[192,256]{1,0:T(8,128)(2,1)}, bf16[48,256]{1,0:T(8,128)(2,1)}) custom-call(bf16[2,192,256]{2,1,0:T(8,128)(2,1)S(1)} %get-tuple-element.76.refs_0_, bf16[2,192,256]{2,1,0:T(8,128)(2,1)S(1)} %collective-permute-done.6.refs_1_, bf16[2,192,256]{2,1,0:T(8,128)(2,1)S(1)} %collective-permute-done.8.refs_2_, ...), custom_call_target="tpu_custom_call" | custom-call | flops 1035000000 | tf_op jit(solution)/shard_map/pallas_call | solution.py:437
  (33 shorter events, 4.0 us)
Async XLA Ops:
  0.6 9.2 %collective-permute-start = (bf16[1,192,256]{2,1,0:T(8,128)(2,1)}, bf16[1,192,256]{2,1,0:T(8,128)(2,1)S(1)}, u32[]{:S(2)}, u32[]{:S(2)}) collective-permute-start(bf16[1,192,256]{2,1,0:T(8,128)(2,1)} %bitcast.3), channel_id=1, source_target_pairs={{0,4},{1,5},{2,6},{3,7},{4,0},{5,1},{6,2},{7,3},{8,12},{9,13},{10,... | collective-permute-start | bytes 294920 | tf_op jit(solution)/shard_map/gather_far/ppermute | solution.py:450
  4.7 3.4 %collective-permute-start.1 = (bf16[48,256]{1,0:T(8,128)(2,1)}, bf16[48,256]{1,0:T(8,128)(2,1)S(1)}, u32[]{:S(2)}, u32[]{:S(2)}) collective-permute-start(bf16[48,256]{1,0:T(8,128)(2,1)} %refs_9_.1), channel_id=1, source_target_pairs={{0,8},{8,0},{16,24},{24,16},{1,9},{9,1},{17,25},{25,17},{2,10},{10... | collective-permute-start | bytes 73736 | tf_op jit(solution)/shard_map/gather_prefix/ppermute | solution.py:450
  4.7 4.9 %collective-permute-start.2 = (bf16[48,256]{1,0:T(8,128)(2,1)}, bf16[48,256]{1,0:T(8,128)(2,1)S(1)}, u32[]{:S(2)}, u32[]{:S(2)}) collective-permute-start(bf16[48,256]{1,0:T(8,128)(2,1)} %refs_9_.1), channel_id=1, source_target_pairs={{0,16},{8,24},{16,0},{24,8},{1,17},{9,25},{17,1},{25,9},{2,18},{10... | collective-permute-start | bytes 73736 | tf_op jit(solution)/shard_map/gather_prefix/ppermute | solution.py:450
  6.3 3.5 %collective-permute-start.3 = (bf16[48,256]{1,0:T(8,128)(2,1)}, bf16[48,256]{1,0:T(8,128)(2,1)S(1)}, u32[]{:S(2)}, u32[]{:S(2)}) collective-permute-start(bf16[48,256]{1,0:T(8,128)(2,1)} %refs_9_.1), channel_id=1, source_target_pairs={{0,24},{8,16},{16,8},{24,0},{1,25},{9,17},{17,9},{25,1},{2,26},{10... | collective-permute-start | bytes 73736 | tf_op jit(solution)/shard_map/gather_prefix/ppermute | solution.py:450
  6.6 5.4 %collective-permute-start.4 = (bf16[1,192,256]{2,1,0:T(8,128)(2,1)}, bf16[1,192,256]{2,1,0:T(8,128)(2,1)S(1)}, u32[]{:S(2)}, u32[]{:S(2)}) collective-permute-start(bf16[1,192,256]{2,1,0:T(8,128)(2,1)} %bitcast.4), channel_id=1, source_target_pairs={{0,2},{1,3},{2,0},{3,1},{4,6},{5,7},{6,4},{7,5},{8,10},{9,11},{10,... | collective-permute-start | bytes 294920 | tf_op jit(solution)/shard_map/gather_near/ppermute | solution.py:450
  8.2 11.8 %collective-permute-start.10 = (bf16[1,192,256]{2,1,0:T(8,128)(2,1)}, bf16[1,192,256]{2,1,0:T(8,128)(2,1)S(1)}, u32[]{:S(2)}, u32[]{:S(2)}) collective-permute-start(bf16[1,192,256]{2,1,0:T(8,128)(2,1)} %bitcast.5), channel_id=1, source_target_pairs={{0,1},{1,0},{2,3},{3,2},{4,5},{5,4},{6,7},{7,6},{8,9},{9,8},{10,11... | collective-permute-start | bytes 294920 | tf_op jit(solution)/shard_map/gather_own_x/ppermute | solution.py:450
  9.9 6.3 %collective-permute-start.9 = (bf16[1,192,256]{2,1,0:T(8,128)(2,1)S(1)}, bf16[1,192,256]{2,1,0:T(8,128)(2,1)S(1)}, u32[]{:S(2)}, u32[]{:S(2)}) collective-permute-start(bf16[1,192,256]{2,1,0:T(8,128)(2,1)S(1)} %collective-permute-done), channel_id=1, source_target_pairs={{0,2},{1,3},{2,0},{3,1},{4,6},{5,7},{6,4},{7,5},{8,10},{9,11},{10,... | collective-permute-start | bytes 294920 | tf_op jit(solution)/shard_map/gather_both/ppermute | solution.py:450
  12.0 7.3 %collective-permute-start.5 = (bf16[2,192,256]{2,1,0:T(8,128)(2,1)S(1)}, bf16[2,192,256]{2,1,0:T(8,128)(2,1)S(1)}, u32[]{:S(2)}, u32[]{:S(2)}) collective-permute-start(bf16[2,192,256]{2,1,0:T(8,128)(2,1)S(1)} %constant_dynamic-update-slice_fusion.refs_4_), channel_id=1, source_target_pairs={{0,1},{1,0},{2,3},{3,2},{4,5},{5,4},{6,7},{7,6},{8,9},{9,8},{10,11... | collective-permute-start | bytes 589832 | tf_op jit(solution)/shard_map/gather_pair_x/ppermute | solution.py:450
  13.6 3.2 %copy-start = (bf16[256,2048]{1,0:T(8,128)(2,1)S(1)}, bf16[256,2048]{1,0:T(8,128)(2,1)}, u32[]{:S(2)}) copy-start(bf16[256,2048]{1,0:T(8,128)(2,1)} %refs_17_.1) | copy-start | bytes 3145732
  16.2 4.7 %collective-permute-start.11 = (bf16[1,192,256]{2,1,0:T(8,128)(2,1)S(1)}, bf16[1,192,256]{2,1,0:T(8,128)(2,1)S(1)}, u32[]{:S(2)}, u32[]{:S(2)}) collective-permute-start(bf16[1,192,256]{2,1,0:T(8,128)(2,1)S(1)} %collective-permute-done.9.refs_5_), channel_id=1, source_target_pairs={{0,1},{1,0},{2,3},{3,2},{4,5},{5,4},{6,7},{7,6},{8,9},{9,8},{10,11... | collective-permute-start | bytes 294920 | tf_op jit(solution)/shard_map/gather_both_x/ppermute | solution.py:450
  17.7 7.9 %collective-permute-start.7 = (bf16[2,192,256]{2,1,0:T(8,128)(2,1)S(1)}, bf16[2,192,256]{2,1,0:T(8,128)(2,1)S(1)}, u32[]{:S(2)}, u32[]{:S(2)}) collective-permute-start(bf16[2,192,256]{2,1,0:T(8,128)(2,1)S(1)} %get-tuple-element.56), channel_id=1, source_target_pairs={{0,2},{1,3},{2,0},{3,1},{4,6},{5,7},{6,4},{7,5},{8,10},{9,11},{10,... | collective-permute-start | bytes 589832 | tf_op jit(solution)/shard_map/out_a/ppermute | solution.py:450
  19.2 15.8 %collective-permute-start.6 = (bf16[2,192,256]{2,1,0:T(8,128)(2,1)S(1)}, bf16[2,192,256]{2,1,0:T(8,128)(2,1)S(1)}, u32[]{:S(2)}, u32[]{:S(2)}) collective-permute-start(bf16[2,192,256]{2,1,0:T(8,128)(2,1)S(1)} %get-tuple-element.54), channel_id=1, source_target_pairs={{0,2},{1,3},{2,0},{3,1},{4,6},{5,7},{6,4},{7,5},{8,10},{9,11},{10,... | collective-permute-start | bytes 589832 | tf_op jit(solution)/shard_map/out_b/ppermute | solution.py:450
  22.7 7.4 %collective-permute-start.13 = (bf16[2,192,256]{2,1,0:T(8,128)(2,1)S(1)}, bf16[2,192,256]{2,1,0:T(8,128)(2,1)S(1)}, u32[]{:S(2)}, u32[]{:S(2)}) collective-permute-start(bf16[2,192,256]{2,1,0:T(8,128)(2,1)S(1)} %get-tuple-element.73), channel_id=1, source_target_pairs={{0,1},{1,0},{2,3},{3,2},{4,5},{5,4},{6,7},{7,6},{8,9},{9,8},{10,11... | collective-permute-start | bytes 589832 | tf_op jit(solution)/shard_map/in_75/ppermute | solution.py:450
  25.7 9.3 %collective-permute-start.8 = (bf16[2,192,256]{2,1,0:T(8,128)(2,1)S(1)}, bf16[2,192,256]{2,1,0:T(8,128)(2,1)S(1)}, u32[]{:S(2)}, u32[]{:S(2)}) collective-permute-start(bf16[2,192,256]{2,1,0:T(8,128)(2,1)S(1)} %add_convert_fusion), channel_id=1, source_target_pairs={{0,4},{1,5},{2,6},{3,7},{4,0},{5,1},{6,2},{7,3},{8,12},{9,13},{10,... | collective-permute-start | bytes 589832 | tf_op jit(solution)/shard_map/out_mid/ppermute | solution.py:450
  28.6 4.7 %collective-permute-start.12 = (bf16[1,192,256]{2,1,0:T(8,128)(2,1)S(1)}, bf16[1,192,256]{2,1,0:T(8,128)(2,1)S(1)}, u32[]{:S(2)}, u32[]{:S(2)}) collective-permute-start(bf16[1,192,256]{2,1,0:T(8,128)(2,1)S(1)} %get-tuple-element.71), channel_id=1, source_target_pairs={{0,1},{1,0},{2,3},{3,2},{4,5},{5,4},{6,7},{7,6},{8,9},{9,8},{10,11... | collective-permute-start | bytes 294920 | tf_op jit(solution)/shard_map/in_3/ppermute | solution.py:450
  30.2 5.5 %collective-permute-start.14 = (bf16[1,192,256]{2,1,0:T(8,128)(2,1)S(1)}, bf16[1,192,256]{2,1,0:T(8,128)(2,1)S(1)}, u32[]{:S(2)}, u32[]{:S(2)}) collective-permute-start(bf16[1,192,256]{2,1,0:T(8,128)(2,1)S(1)} %add_convert_fusion.3), channel_id=1, source_target_pairs={{0,2},{1,3},{2,0},{3,1},{4,6},{5,7},{6,4},{7,5},{8,10},{9,11},{10,... | collective-permute-start | bytes 294920 | tf_op jit(solution)/shard_map/in_6/ppermute | solution.py:450
  33.3 8.3 %collective-permute-start.17 = (bf16[1,192,256]{2,1,0:T(8,128)(2,1)S(1)}, bf16[1,192,256]{2,1,0:T(8,128)(2,1)S(1)}, u32[]{:S(2)}, u32[]{:S(2)}) collective-permute-start(bf16[1,192,256]{2,1,0:T(8,128)(2,1)S(1)} %add_convert_fusion.4), channel_id=1, source_target_pairs={{0,2},{1,3},{2,0},{3,1},{4,6},{5,7},{6,4},{7,5},{8,10},{9,11},{10,... | collective-permute-start | bytes 294920 | tf_op jit(solution)/shard_map/in_2/ppermute | solution.py:450
  35.0 4.9 %collective-permute-start.19 = (f32[2,48,256]{2,1,0:T(8,128)S(1)}, f32[2,48,256]{2,1,0:T(8,128)S(1)}, u32[]{:S(2)}, u32[]{:S(2)}) collective-permute-start(f32[2,48,256]{2,1,0:T(8,128)S(1)} %get-tuple-element.82), channel_id=1, source_target_pairs={{0,8},{8,0},{16,24},{24,16},{1,9},{9,1},{17,25},{25,17},{2,10},{10... | collective-permute-start | bytes 294920 | tf_op jit(solution)/shard_map/grad_prefix_core/ppermute | solution.py:450
  35.7 8.3 %collective-permute-start.18 = (bf16[1,192,256]{2,1,0:T(8,128)(2,1)S(1)}, bf16[1,192,256]{2,1,0:T(8,128)(2,1)S(1)}, u32[]{:S(2)}, u32[]{:S(2)}) collective-permute-start(bf16[1,192,256]{2,1,0:T(8,128)(2,1)S(1)} %add_convert_fusion.2), channel_id=1, source_target_pairs={{0,4},{1,5},{2,6},{3,7},{4,0},{5,1},{6,2},{7,3},{8,12},{9,13},{10,... | collective-permute-start | bytes 294920 | tf_op jit(solution)/shard_map/in_4/ppermute | solution.py:450
  37.8 6.3 %collective-permute-start.15 = (bf16[1,192,256]{2,1,0:T(8,128)(2,1)S(1)}, bf16[1,192,256]{2,1,0:T(8,128)(2,1)S(1)}, u32[]{:S(2)}, u32[]{:S(2)}) collective-permute-start(bf16[1,192,256]{2,1,0:T(8,128)(2,1)S(1)} %add_convert_fusion.1), channel_id=1, source_target_pairs={{0,1},{1,0},{2,3},{3,2},{4,5},{5,4},{6,7},{7,6},{8,9},{9,8},{10,11... | collective-permute-start | bytes 294920 | tf_op jit(solution)/shard_map/out_x/ppermute | solution.py:450
  39.1 4.9 %collective-permute-start.16 = (bf16[1,192,256]{2,1,0:T(8,128)(2,1)S(1)}, bf16[1,192,256]{2,1,0:T(8,128)(2,1)S(1)}, u32[]{:S(2)}, u32[]{:S(2)}) collective-permute-start(bf16[1,192,256]{2,1,0:T(8,128)(2,1)S(1)} %get-tuple-element.79), channel_id=1, source_target_pairs={{0,1},{1,0},{2,3},{3,2},{4,5},{5,4},{6,7},{7,6},{8,9},{9,8},{10,11... | collective-permute-start | bytes 294920 | tf_op jit(solution)/shard_map/in_1/ppermute | solution.py:450
  39.9 4.2 %collective-permute-start.20 = (f32[1,48,256]{2,1,0:T(8,128)S(1)}, f32[1,48,256]{2,1,0:T(8,128)S(1)}, u32[]{:S(2)}, u32[]{:S(2)}) collective-permute-start(f32[1,48,256]{2,1,0:T(8,128)S(1)} %slice_add_fusion), channel_id=1, source_target_pairs={{0,16},{8,24},{16,0},{24,8},{1,17},{9,25},{17,1},{25,9},{2,18},{10... | collective-permute-start | bytes 147464 | tf_op jit(solution)/shard_map/grad_prefix_y/ppermute | solution.py:450
